TPU v7x, 512 devices: a whole 4x4x16 slice. The times are simulated.
512 devices in a mesh: replica: 4 (over x), vocab: 16 (over z_lo, core), dp: 8 (over z_hi, y).
Axes of the slice: x: 4, y: 4, z: 16 (z_hi: 2, z_lo: 8; z = z_hi * 8 + z_lo), core: 2. Of those that a mesh axis runs over, the one named last changes fastest.
Arguments:
- hidden: bfloat16 [4, 512, 1792], P('replica', 'dp'), may hold values from -16 to 16
- head_weight: bfloat16 [4, 1792, 131072], P('replica', None, ('vocab', 'dp')), may hold values from -1 to 1
- targets: int32 [512], P('dp'), may hold values from 0 to 131071
- pairing: int32 [4], replicated, may hold values from 0 to 3, as said below
- token_weight: float32 [4, 512], P('replica', 'dp'), may hold values from 1 to 10
Outputs:
- grad_hidden: bfloat16 [4, 512, 1792], P('replica', 'dp')
- token_loss: float32 [4, 512], P('replica', 'dp')
Inputs may be any that keep to these rules, and one draw needn't show every extreme that they name: pairing[r] is the replica whose predictions replica r learns from; following pairing from any replica visits all four replicas once before returning, and one of its steps goes to the replica two indices away.
All inputs are finite; a program needn't handle non-finite values.
Results may differ from a plain program's by a relative error of at most 0.015.
Values may be sent and summed in bfloat16 or wider, within the bound.
No kernel may reach another device: no remote copies, remote signals or barrier semaphores. Data moves between devices by JAX's collectives and lax.ppermute only.
A program may use at most 64 MiB of HBM per device.

v0:
```python
import jax
import jax.numpy as jnp
from jax import lax
from jax.sharding import PartitionSpec as P

kl_weight = 1.0


def on_device(hidden, head_weight, targets, pairing, token_weight):
    tok_rows = hidden.shape[1]
    gathered_hidden, all_targets, all_weights = (
        lax.all_gather(hidden, "dp", axis=1, tiled=True),
        lax.all_gather(targets, "dp", axis=0, tiled=True),
        lax.all_gather(token_weight.astype(jnp.bfloat16), "dp", axis=1, tiled=True).astype(
            token_weight.dtype
        ),
    )
    hidden_rows = gathered_hidden[0]
    weights = all_weights[0]
    head_rows = head_weight[0]
    vocab_cols = head_rows.shape[1]
    offset = lax.axis_index(("vocab", "dp")) * vocab_cols
    logits = jnp.dot(hidden_rows, head_rows, preferred_element_type=jnp.float32)
    columns = jnp.arange(vocab_cols, dtype=jnp.int32)
    onehot = (columns[None, :] == (all_targets - offset)[:, None]).astype(jnp.float32)
    local_target = jnp.sum(logits * onehot, axis=1)
    local_top = jnp.max(logits, axis=1)
    row_top = lax.pmax(local_top, ("vocab", "dp"))
    local_total = jnp.sum(jnp.exp(logits - row_top[:, None]), axis=1)
    row_total, target_logit = lax.psum((local_total, local_target), ("vocab", "dp"))
    log_total = row_top + jnp.log(row_total)
    own_logp = logits - log_total[:, None]
    own_prob = jnp.exp(own_logp)
    gathered_logp = lax.all_gather(own_logp[None], "replica", axis=0, tiled=True)
    replica_ids = jnp.arange(pairing.shape[0], dtype=jnp.int32)
    partner = jnp.sum(jnp.where(replica_ids == lax.axis_index("replica"), pairing, 0))
    peer_logp = lax.dynamic_index_in_dim(gathered_logp, partner, 0, keepdims=False)
    peer_prob = jnp.exp(peer_logp)
    log_ratio = own_logp - peer_logp
    kl_forward, kl_reverse = lax.psum(
        (jnp.sum(peer_prob * -log_ratio, axis=1), jnp.sum(own_prob * log_ratio, axis=1)),
        ("vocab", "dp"),
    )
    losses = weights * (log_total - target_logit + 0.5 * kl_weight * (kl_forward + kl_reverse))
    own_losses = lax.dynamic_slice_in_dim(losses, lax.axis_index("dp") * tok_rows, tok_rows, 0)
    inner = (
        own_prob
        - onehot
        + 0.5 * kl_weight * (own_prob - peer_prob + own_prob * (log_ratio - kl_reverse[:, None]))
    )
    logit_grad = (weights[:, None] * inner).astype(jnp.bfloat16)
    partial_grad = lax.psum_scatter(
        lax.dot_general(
            logit_grad, head_rows, (((1,), (1,)), ((), ())), preferred_element_type=jnp.float32
        ),
        "dp",
        scatter_dimension=0,
        tiled=True,
    )
    grads = lax.psum(partial_grad, "vocab").astype(jnp.bfloat16)
    return (grads[None], own_losses[None])


def solution(mesh):
    return jax.shard_map(
        on_device,
        mesh=mesh,
        in_specs=(
            P("replica", "dp", None),
            P("replica", None, ("vocab", "dp")),
            P("dp"),
            P(),
            P("replica", "dp"),
        ),
        out_specs=(P("replica", "dp", None), P("replica", "dp")),
        check_vma=False,
    )
```

profile of v0, /device:TPU:1, one launch (start us, length us, event | category | flops | bytes accessed | tf_op | source)
XLA Modules:
  0.0 2085.8 jit_solution(16005323297353087711)
XLA Ops:
  7.2 0.0 all-gather.4.cloned.1.call-start
  7.2 0.7 all-gather.4.cloned.1.call-update
  7.9 0.0 all-gather.6.cloned.1.call-start
  8.0 1.3 dynamic-slice
  9.9 0.9 dynamic-update-slice.1
  10.7 22.4 %all-reduce.1 = s32[512]{0:T(512)S(1)} all-reduce(s32[512]{0:T(512)S(1)} %dynamic-update-slice.1), channel_id=1, replica_groups=mesh['replica'=4,'vocab'=16,'dp'=8] {'dp'}, use_global_device_ids=true, to_apply=%add.1 | all-reduce | flops 512 | bytes 4096
  33.1 92.9 %all-gather.4.cloned.1.call-done = bf16[1,512,1792]{2,1,0:T(8,128)(2,1)} async-done(((bf16[1,64,1792]{2,1,0:T(8,128)(2,1)}), bf16[1,512,1792]{2,1,0:T(8,128)(2,1)}) %all-gather.4.cloned.1.call-update) | async-done | bytes 1835024 | tf_op jit(solution)/shard_map/all_gather | solution.py:12
  126.0 4.7 fusion.12
  130.8 506.5 %pmax.7 = f32[512]{0:T(512)S(1)} all-reduce(f32[512]{0:T(512)S(1)} %get-tuple-element.9), channel_id=1, replica_groups=mesh['replica'=4,'vocab'=16,'dp'=8] {'vocab','dp'}, use_global_device_ids=true, to_apply=%region_1.0 | all-reduce | flops 512 | bytes 4096 | tf_op jit(solution)/shard_map/pmax | solution.py:28
  637.3 0.8 select_reduce_fusion
  638.1 514.7 %psum.35 = f32[512]{0:T(512)S(1)} all-reduce(f32[512]{0:T(512)S(1)} %get-tuple-element.5), channel_id=1, replica_groups=mesh['replica'=4,'vocab'=16,'dp'=8] {'vocab','dp'}, use_global_device_ids=true, to_apply=%region_3.0 | all-reduce | flops 512 | bytes 4096 | tf_op jit(solution)/shard_map/psum | solution.py:30
  1152.9 1.6 broadcast_subtract_fusion
  1154.5 0.0 reduce-scatter.2.cloned.1.call-start
  1154.5 0.6 copy-done
  1155.1 0.6 fusion.9
  1157.1 0.2 dynamic-update-slice
  1157.3 30.8 %all-reduce = bf16[512]{0:T(512)(128)(2,1)S(1)} all-reduce(bf16[512]{0:T(512)(128)(2,1)S(1)} %dynamic-update-slice), channel_id=1, replica_groups=mesh['replica'=4,'vocab'=16,'dp'=8] {'dp'}, use_global_device_ids=true, to_apply=%add | all-reduce | flops 512 | bytes 2048
  1188.8 69.6 %all-gather.6.cloned.1.call-done = f32[2048,1024]{1,0:T(8,128)} async-done(((f32[512,1024]{1,0:T(8,128)}), f32[2048,1024]{1,0:T(8,128)}) %all-gather.6.cloned.1.call-update) | async-done | bytes 8388624 | tf_op jit(solution)/shard_map/all_gather | solution.py:34
  1258.3 2.6 multiply_reduce_fusion
  1260.9 510.3 %all-reduce.2 = (f32[512]{0:T(512)S(1)}, f32[512]{0:T(512)S(1)}, f32[512]{0:T(512)S(1)}) all-reduce(f32[512]{0:T(512)S(1)} %get-tuple-element.3, f32[512]{0:T(512)S(1)} %get-tuple-element.2, f32[512]{0:T(512)S(1)} %get-tuple-element.4), channel_id=1, replica_groups=mesh['replica'=4,'vocab'=16,'dp'=8] {'vocab','dp'}, use_global_device_ids=true, to_apply=%region_6.7 | all-reduce | flops 1536 | bytes 12288 | tf_op jit(solution)/shard_map/psum | solution.py:40
  1771.2 8.2 fusion
  1779.4 0.6 dynamic-slice_bitcast_fusion
  1780.0 211.6 %reduce-scatter.2.cloned.1.call-done = f32[64,1792]{1,0:T(8,128)} async-done(((f32[512,1792]{1,0:T(8,128)}), f32[64,1792]{1,0:T(8,128)}) %reduce-scatter.2.cloned.1.call-update) | async-done | bytes 458768 | tf_op jit(solution)/shard_map/reduce_scatter | solution.py:52
  1991.6 87.7 %all-reduce.4 = bf16[64,1792]{1,0:T(8,128)(2,1)} all-reduce(f32[64,1792]{1,0:T(8,128)} %reduce-scatter.2.cloned.1.call-done), channel_id=1, replica_groups=mesh['replica'=4,'vocab'=16,'dp'=8] {'vocab'}, use_global_device_ids=true, to_apply=%region_8.9 | all-reduce | flops 114688 | bytes 688128 | tf_op jit(solution)/shard_map/psum | solution.py:60
  (12 shorter events, 0.1 us)
Async XLA Ops:
  7.2 118.9 %all-gather.4.cloned.1.call-start = ((), (), s32[]{:S(2)}) async-start(), calls=%async_computation.1 | async-start | bytes 2064384 | tf_op jit(solution)/shard_map/all_gather | solution.py:12
  7.9 1250.4 %all-gather.6.cloned.1.call-start = ((), (), s32[]{:S(2)}) async-start(), calls=%async_computation.3 | async-start | bytes 10485760 | tf_op jit(solution)/shard_map/all_gather | solution.py:34
  1154.5 0.7 copy-start
  1154.5 2.6 copy-start.1
  1154.5 837.1 %reduce-scatter.2.cloned.1.call-start = ((), (), s32[]{:S(2)}) async-start(), calls=%async_computation.2 | async-start | bytes 4128768 | tf_op jit(solution)/shard_map/reduce_scatter | solution.py:52
Sparse Core Ops, SparseCore 0:
  11.2 114.8 all-gather.3
  1154.6 103.6 all-gather.5
  1779.5 212.0 reduce-scatter.1
where the time goes:
time: 2090 us
  blocking collectives  1670 us (80%)
  waiting for transfers between devices  375 us (18%)
    psum x1, blocking collectives, on_device(): lax.psum((local_total, local_target), ('vocab', 'dp'))  515 us
    psum x1, blocking collectives, on_device(): lax.psum((jnp.sum(peer_prob * -log_ratio, axis=1), jnp.sum(own_prob * log...  510 us
    pmax x1, blocking collectives, on_device(): row_top = lax.pmax(local_top, ('vocab', 'dp'))  507 us
    reduce_scatter x1, waiting for transfers between devices, on_device(): lax.psum_scatter(lax.dot_general(logit_grad, head_rows, (((1,), (1,)), ((...  212 us
    all_gather x1, waiting for transfers between devices, on_device(): lax.all_gather(hidden, 'dp', axis=1, tiled=True)  92.9 us
    psum x1, blocking collectives, on_device(): grads = lax.psum(partial_grad, 'vocab').astype(jnp.bfloat16)  87.7 us
    all_gather x1, waiting for transfers between devices, on_device(): lax.all_gather(own_logp[None], 'replica', axis=0, tiled=True)  69.6 us
    unnamed x2, blocking collectives  53.2 us
  transfers between devices with their start and end apart: 3, of which 3 were waited for; matrix products, arithmetic and copies ran while one was open for 0% of the time, Pallas kernels for 0%

commit v1 on v0

v1 whole, which is shorter than its diff:
```python
import functools

import jax
import jax.numpy as jnp
from jax import lax
from jax.experimental import pallas as pl
from jax.experimental.pallas import tpu as pltpu
from jax.sharding import Mesh
from jax.sharding import PartitionSpec as P

kl_weight = 1.0
F32 = jnp.float32
BF16 = jnp.bfloat16
R = 4
Z = ("zh", "zl")
FAR = {0: 12, 1: 13, 2: 14, 3: 15, 4: 8, 5: 9, 6: 10, 7: 11}
FAR.update({b: a for a, b in FAR.items()})
SWAP_Z = [(z % 8 * 2 + z // 8, FAR[z] % 8 * 2 + FAR[z] // 8) for z in range(16)]
SWAP_C = [(0, 1), (1, 0)]


def forward_kernel(half_ref, mine_ref, other_ref, w_mine_ref, w_other_ref, out_ref):
    depth = w_mine_ref.shape[1]
    out_ref[...] = jnp.dot(
        mine_ref[:, :depth], w_mine_ref[0], preferred_element_type=F32
    ) + jnp.dot(other_ref[:, :depth], w_other_ref[0], preferred_element_type=F32)


def forward(half, mine, other, head):
    rows, depth, cols = mine.shape[0], head.shape[1] // 2, head.shape[2]
    tile = 256
    return pl.pallas_call(
        forward_kernel,
        out_shape=jax.ShapeDtypeStruct((rows, cols), F32),
        grid_spec=pltpu.PrefetchScalarGridSpec(
            num_scalar_prefetch=1,
            grid=(cols // tile,),
            in_specs=[
                pl.BlockSpec(mine.shape, lambda n, h: (0, 0)),
                pl.BlockSpec(other.shape, lambda n, h: (0, 0)),
                pl.BlockSpec((1, depth, tile), lambda n, h: (0, h[0], n)),
                pl.BlockSpec((1, depth, tile), lambda n, h: (0, 1 - h[0], n)),
            ],
            out_specs=pl.BlockSpec((rows, tile), lambda n, h: (0, n)),
        ),
        compiler_params=pltpu.CompilerParams(vmem_limit_bytes=40 << 20),
        name="logits",
    )(half, mine, other, head, head)


def stats_kernel(pair_ref, tgt_ref, l_ref, out_ref, cols_ref):
    step = pl.program_id(0)
    rows, vocab = l_ref.shape[1], l_ref.shape[2]
    lane = lax.broadcasted_iota(jnp.int32, (rows, 128), 1)
    hit = lax.broadcasted_iota(jnp.int32, (rows, vocab), 1) == tgt_ref[...]
    for r in range(R):
        learner = jnp.int32(0)
        for k in range(R):
            learner = jnp.where(pair_ref[k] == r, k, learner)
        logits = l_ref[r]
        top = jnp.max(logits, axis=1, keepdims=True)
        power = jnp.exp(logits - top)
        total = jnp.sum(power, axis=1, keepdims=True)
        to_peer = jnp.sum(power * (logits - l_ref[pair_ref[r]]), axis=1, keepdims=True)
        to_learner = jnp.sum(power * (logits - l_ref[learner]), axis=1, keepdims=True)
        target = jnp.sum(jnp.where(hit, logits, 0.0), axis=1, keepdims=True)
        packed = jnp.zeros((rows, 128), F32)
        for i, v in enumerate((top, total, to_peer, to_learner, target)):
            packed = jnp.where(lane == i, v, packed)
        cols_ref[r, pl.ds(pl.multiple_of(step * rows, rows), rows), :] = packed

    @pl.when(step == pl.num_programs(0) - 1)
    def _():
        for r in range(R):
            flat = jnp.transpose(cols_ref[r])[:8]
            for k in range(out_ref.shape[0]):
                out_ref[k, r] = flat


def stats(pairing, tgt, logits, copies):
    rows, vocab = logits.shape[1], logits.shape[2]
    tile = 32
    return pl.pallas_call(
        stats_kernel,
        out_shape=jax.ShapeDtypeStruct((copies, R, 8, rows), F32),
        grid_spec=pltpu.PrefetchScalarGridSpec(
            num_scalar_prefetch=1,
            grid=(rows // tile,),
            in_specs=[
                pl.BlockSpec((tile, 1), lambda n, p: (n, 0)),
                pl.BlockSpec((R, tile, vocab), lambda n, p: (0, n, 0)),
            ],
            out_specs=pl.BlockSpec((copies, R, 8, rows), lambda n, p: (0, 0, 0, 0)),
            scratch_shapes=[pltpu.VMEM((R, rows, 128), F32)],
        ),
        compiler_params=pltpu.CompilerParams(vmem_limit_bytes=24 << 20),
        name="local_stats",
    )(pairing, tgt, logits)


def merged(parts):
    top = jnp.max(parts[:, :, 0], axis=0)
    scale = jnp.exp(parts[:, :, 0] - top[None])
    sums = [jnp.sum(parts[:, :, i] * scale, axis=0) for i in (1, 2, 3)]
    return [top] + sums + [jnp.sum(parts[:, :, 4], axis=0)]


def merge_kernel(in_ref, out_ref):
    values = merged(in_ref[...])
    for k in range(out_ref.shape[0]):
        for i, v in enumerate(values):
            out_ref[k, :, i, :] = v
        for i in range(len(values), 8):
            out_ref[k, :, i, :] = jnp.zeros_like(values[0])


def merge(parts, copies):
    return pl.pallas_call(
        merge_kernel,
        out_shape=jax.ShapeDtypeStruct((copies,) + parts.shape[1:], F32),
        compiler_params=pltpu.CompilerParams(vmem_limit_bytes=24 << 20),
        name="merge_stats",
    )(parts)


def grad_kernel(pair_ref, parts_ref, tgt_ref, l_ref, out_ref, flat_ref, cols_ref, prob_ref):
    step = pl.program_id(0)
    last = pl.num_programs(0) - 1
    rows, vocab = l_ref.shape[1], l_ref.shape[2]

    @pl.when(step == 0)
    def _():
        top, total, to_peer, to_learner, target = merged(parts_ref[...])
        log_total = top + jnp.log(total)
        flat_ref[...] = jnp.zeros_like(flat_ref)
        flat_ref[:, 0, :] = log_total
        flat_ref[:, 4, :] = to_peer / total
        flat_ref[:, 5, :] = to_learner / total
        flat_ref[:, 6, :] = target
        for r in range(R):
            peer = pair_ref[r]
            own_total, peer_total = flat_ref[r, 0:1, :], flat_ref[peer, 0:1, :]
            reverse = flat_ref[r, 4:5, :] - (own_total - peer_total)
            forward_kl = flat_ref[peer, 5:6, :] - (peer_total - own_total)
            flat_ref[r, 1:2, :] = peer_total
            flat_ref[r, 2:3, :] = reverse
            flat_ref[r, 3:4, :] = (
                own_total - flat_ref[r, 6:7, :] + 0.5 * kl_weight * (forward_kl + reverse)
            )
        for r in range(R):
            cols_ref[r] = jnp.transpose(flat_ref[r])

    @pl.when(step < last)
    def _():
        at = pl.ds(pl.multiple_of(step * rows, rows), rows)
        hit = lax.broadcasted_iota(jnp.int32, (rows, vocab), 1) == tgt_ref[...]
        onehot = jnp.where(hit, 1.0, 0.0)
        for r in range(R):
            prob_ref[r] = jnp.exp(l_ref[r] - cols_ref[r, at, 0:1])
        for r in range(R):
            peer = pair_ref[r]
            own_prob = prob_ref[r]
            ratio = (l_ref[r] - cols_ref[r, at, 0:1]) - (l_ref[peer] - cols_ref[r, at, 1:2])
            inner = (
                own_prob
                - onehot
                + 0.5
                * kl_weight
                * ((own_prob - prob_ref[peer]) + own_prob * (ratio - cols_ref[r, at, 2:3]))
            )
            out_ref[r] = inner.astype(BF16)

    @pl.when(step == last)
    def _():
        out_ref[...] = jnp.zeros_like(out_ref)
        row = lax.broadcasted_iota(jnp.int32, (out_ref.shape[1], 128), 0)
        for r in range(R):
            loss = flat_ref[r, 3:4, :]
            high = loss.astype(BF16).astype(F32)
            middle = (loss - high).astype(BF16).astype(F32)
            low = (loss - high) - middle
            pieces = jnp.where(
                row == 0, high, jnp.where(row == 1, middle, jnp.where(row == 2, low, 0.0))
            )
            out_ref[r, :, 0:128] = pieces.astype(BF16)


def logit_grads(pairing, parts, tgt, logits):
    rows, vocab = logits.shape[1], logits.shape[2]
    tile = 16
    steps = rows // tile
    return pl.pallas_call(
        grad_kernel,
        out_shape=jax.ShapeDtypeStruct((R, rows + tile, vocab), BF16),
        grid_spec=pltpu.PrefetchScalarGridSpec(
            num_scalar_prefetch=1,
            grid=(steps + 1,),
            in_specs=[
                pl.BlockSpec(parts.shape, lambda n, p: (0, 0, 0, 0)),
                pl.BlockSpec((tile, 1), lambda n, p: (jnp.minimum(n, steps - 1), 0)),
                pl.BlockSpec((R, tile, vocab), lambda n, p: (0, jnp.minimum(n, steps - 1), 0)),
            ],
            out_specs=pl.BlockSpec((R, tile, vocab), lambda n, p: (0, n, 0)),
            scratch_shapes=[
                pltpu.VMEM((R, 128, 128), F32),
                pltpu.VMEM((R, 128, 128), F32),
                pltpu.VMEM((R, tile, vocab), F32),
            ],
        ),
        compiler_params=pltpu.CompilerParams(vmem_limit_bytes=24 << 20),
        name="logit_grads",
    )(pairing, parts, tgt, logits)


def backward_kernel(half_ref, g_ref, w_ref, out_ref):
    part = g_ref.shape[1] - 16
    g = g_ref[:, :part, :].reshape(R * part, g_ref.shape[2])
    out_ref[...] = lax.dot_general(
        g, w_ref[0], (((1,), (1,)), ((), ())), preferred_element_type=F32
    ).astype(out_ref.dtype)


def backward(half, grads, head, dtype):
    rows, depth, cols = R * (grads.shape[1] - 16), head.shape[1] // 2, head.shape[2]
    tile = 128
    tiles = depth // tile
    return pl.pallas_call(
        backward_kernel,
        out_shape=jax.ShapeDtypeStruct((rows, depth), dtype),
        grid_spec=pltpu.PrefetchScalarGridSpec(
            num_scalar_prefetch=1,
            grid=(tiles,),
            in_specs=[
                pl.BlockSpec(grads.shape, lambda n, h: (0, 0, 0)),
                pl.BlockSpec((1, tile, cols), lambda n, h: (0, h[0] * tiles + n, 0)),
            ],
            out_specs=pl.BlockSpec((rows, tile), lambda n, h: (0, n)),
        ),
        compiler_params=pltpu.CompilerParams(vmem_limit_bytes=40 << 20),
        name="head_grads",
    )(half, grads, head)


def on_device(hidden, head_weight, targets, pairing, token_weight):
    x, zl, c, zh, y = (lax.axis_index(a) for a in ("x", "zl", "c", "zh", "y"))
    rows, features = hidden.shape[1], hidden.shape[2]
    depth = features // 2
    vocab = head_weight.shape[2]
    offset = (((zl * 2 + c) * 2 + zh) * 4 + y) * vocab
    half = c.reshape(1)

    ids = jnp.stack([targets >> 12, (targets >> 6) & 63, targets & 63], axis=1).astype(BF16)
    mine = jnp.concatenate(
        [
            lax.dynamic_slice_in_dim(hidden[0], c * depth, depth, 1),
            jnp.pad(ids, ((0, 0), (0, 125))),
        ],
        axis=1,
    )
    far = lax.ppermute(mine, ("zl", "zh"), SWAP_Z)
    both = jnp.where(zh == 0, jnp.stack([mine, far]), jnp.stack([far, mine]))
    both = both.reshape(2 * rows, depth + 128)
    all_mine = lax.all_to_all(jnp.broadcast_to(both[None], (4,) + both.shape), "y", 0, 0)
    all_mine = all_mine.reshape(8 * rows, depth + 128)
    all_other = lax.ppermute(all_mine, "c", SWAP_C)

    logits = forward(half, all_mine, all_other, head_weight).reshape(R, 2 * rows, vocab)
    sources = lax.all_to_all(logits, "x", 0, 0)
    ids = lax.dynamic_slice(all_mine, (x * 2 * rows, depth), (2 * rows, 3)).astype(jnp.int32)
    tgt = ((ids[:, 0:1] << 12) | (ids[:, 1:2] << 6) | ids[:, 2:3]) - offset

    local = stats(pairing, tgt, sources, 8)
    near = merge(lax.all_to_all(local, ("c", "y"), 0, 0), 16)
    parts = lax.all_to_all(near, Z, 0, 0)
    grads = lax.all_to_all(logit_grads(pairing, parts, tgt, sources), "x", 0, 0)

    loss = lax.dynamic_slice(grads, (y, 2 * rows, zh * rows), (1, 3, rows))[0].astype(F32)
    losses = token_weight[0] * (loss[0] + (loss[1] + loss[2]))

    sent = lax.ppermute(backward(1 - half, grads, head_weight, BF16), "c", SWAP_C)
    kept = backward(half, grads, head_weight, F32)
    by_y = (kept + sent.astype(F32)).astype(BF16).reshape(4, 2 * rows, depth)
    by_y = lax.all_to_all(by_y, "y", 0, 0)
    by_z = jnp.sum(by_y.astype(F32), axis=0).astype(BF16).reshape(16, rows // 8, depth)
    by_z = lax.all_to_all(by_z, Z, 0, 0)
    weights = lax.dynamic_slice_in_dim(token_weight[0], zl * (rows // 8), rows // 8, 0)
    final = (jnp.sum(by_z.astype(F32), axis=0) * weights[:, None]).astype(BF16)
    final = lax.all_to_all(
        jnp.broadcast_to(final[None], (16,) + final.shape), ("zl", "c"), 0, 0
    )
    final = final.reshape(8, 2, rows // 8, depth).transpose(0, 2, 1, 3).reshape(rows, features)
    return (final[None], losses[None])


def solution(mesh):
    fine = Mesh(mesh.devices.reshape(4, 8, 2, 2, 4), ("x", "zl", "c", "zh", "y"))
    return jax.shard_map(
        on_device,
        mesh=fine,
        in_specs=(
            P("x", ("zh", "y"), None),
            P("x", None, ("zl", "c", "zh", "y")),
            P(("zh", "y")),
            P(),
            P("x", ("zh", "y")),
        ),
        out_specs=(P("x", ("zh", "y"), None), P("x", ("zh", "y"))),
        check_vma=False,
    )
```

time: 2090 us -> 225 us (0.11)
  blocking collectives: 1670 us -> 65.7 us
  waiting for transfers between devices: 375 us -> 77.7 us
  starting transfers between devices: 0.12 us -> 55.1 us
    psum x3 -> x0, blocking collectives: 1110 us -> none  [the longest x1 515 us: on_device(): lax.psum((local_total, local_target), ('vocab', 'dp'))]
    pmax x1 -> x0, blocking collectives: 507 us -> none  [on_device(): row_top = lax.pmax(local_top, ('vocab', 'dp'))]
    reduce_scatter x1 -> x0, waiting for transfers between devices: 212 us -> none  [on_device(): lax.psum_scatter(lax.dot_general(logit_grad, head_rows, (((1,), (1,)), ((...]
    all_gather x2 -> x0, waiting for transfers between devices: 162 us -> none  [the longest x1 92.9 us: on_device(): lax.all_gather(hidden, 'dp', axis=1, tiled=True)]
    all_to_all x0 -> x4, blocking collectives: none -> 65.7 us  [the longest x1 22.8 us: on_device(): parts = lax.all_to_all(near, Z, 0, 0)]
    all_to_all x0 -> x4, waiting for transfers between devices: none -> 64.3 us  [the longest x1 25.6 us: on_device(): sources = lax.all_to_all(logits, 'x', 0, 0)]
    unnamed x2 -> x0, blocking collectives: 53.2 us -> none
    all_to_all x0 -> x4, starting transfers between devices: none -> 29 us  [the longest x1 11 us: on_device(): lax.all_to_all(jnp.broadcast_to(final[None], (16,) + final.shape), ('zl',...]
  transfers between devices with their start and end apart: 3 -> 7, of which waited for: 3 -> 6; matrix products, arithmetic and copies ran while one was open for 0% -> 0% of each run, Pallas kernels for 0% -> 1%
where the time goes in v1:
time: 225 us
  waiting for transfers between devices  77.7 us (35%)
  blocking collectives  65.7 us (29%)
  starting transfers between devices  55.1 us (24%)
  Pallas kernels  17.7 us (8%)
  local copies, waits for them, and re-layouts  5.22 us (2%)
  other arithmetic  2.6 us (1%)
    all_to_all x1, waiting for transfers between devices, on_device(): sources = lax.all_to_all(logits, 'x', 0, 0)  25.6 us
    all_to_all x1, blocking collectives, on_device(): parts = lax.all_to_all(near, Z, 0, 0)  22.8 us
    all_to_all x1, blocking collectives, on_device(): lax.all_to_all(jnp.broadcast_to(both[None], (4,) + both.shape), 'y', 0, 0)  17.8 us
    all_to_all x1, blocking collectives, on_device(): by_y = lax.all_to_all(by_y, 'y', 0, 0)  16 us
    all_to_all x1, waiting for transfers between devices, on_device(): lax.all_to_all(jnp.broadcast_to(final[None], (16,) + final.shape), ('zl',...  15.2 us
    ppermute x1, starting transfers between devices, on_device(): far = lax.ppermute(mine, ('zl', 'zh'), SWAP_Z)  13.3 us
    all_to_all x1, waiting for transfers between devices, on_device(): by_z = lax.all_to_all(by_z, Z, 0, 0)  12.5 us
    ppermute x1, waiting for transfers between devices, on_device(): far = lax.ppermute(mine, ('zl', 'zh'), SWAP_Z)  11.1 us
  transfers between devices with their start and end apart: 7, of which 6 were waited for; matrix products, arithmetic and copies ran while one was open for 0% of the time, Pallas kernels for 1%

profile of v1, /device:TPU:1, one launch (start us, length us, event | category | flops | bytes accessed | tf_op | source)
XLA Modules:
  0.0 224.8 jit_solution(7070036575064344814)
XLA Ops:
  1.6 13.3 %collective-permute-start = (bf16[64,1024]{1,0:T(8,128)(2,1)S(1)}, bf16[64,1024]{1,0:T(8,128)(2,1)S(1)}, u32[]{:S(2)}, u32[]{:S(2)}) collective-permute-start(bf16[64,1024]{1,0:T(8,128)(2,1)S(1)} %get-tuple-element.3), channel_id=1, source_target_pairs={{0,68},{16,84},{32,100},{48,116},{64,4},{80,20},{96,36},{112,52},{... | collective-permute-start | bytes 393224 | tf_op jit(solution)/shard_map/ppermute | solution.py:260
  14.9 11.1 %collective-permute-done = bf16[64,1024]{1,0:T(8,128)(2,1)S(1)} collective-permute-done((bf16[64,1024]{1,0:T(8,128)(2,1)S(1)}, bf16[64,1024]{1,0:T(8,128)(2,1)S(1)}, u32[]{:S(2)}, u32[]{:S(2)}) %collective-permute-start) | collective-permute-done | bytes 131104 | tf_op jit(solution)/shard_map/ppermute | solution.py:260
  26.2 17.8 %all_to_all.40 = bf16[4,128,1024]{2,1,0:T(8,128)(2,1)S(1)} all-to-all(bf16[4,128,1024]{2,1,0:T(8,128)(2,1)S(1)} %broadcast_in_dim.4), channel_id=1, replica_groups=mesh['x'=4,'zl'=8,'c'=2,'zh'=2,'y'=4] {'y'}, dimensions={0} | all-to-all | bytes 2097152 | tf_op jit(solution)/shard_map/all_to_all | solution.py:263
  44.1 4.4 %collective-permute-start.1 = (bf16[512,1024]{1,0:T(8,128)(2,1)S(1)}, bf16[512,1024]{1,0:T(8,128)(2,1)S(1)}, u32[]{:S(2)}, u32[]{:S(2)}) collective-permute-start(bf16[512,1024]{1,0:T(8,128)(2,1)S(1)} %bitcast.27), channel_id=1, source_target_pairs={{0,8},{8,0},{1,9},{9,1},{2,10},{10,2},{3,11},{11,3},{4,12},{12,4},... | collective-permute-start | bytes 3145736 | tf_op jit(solution)/shard_map/ppermute | solution.py:265
  48.4 2.3 %collective-permute-done.1.other_ref = bf16[512,1024]{1,0:T(8,128)(2,1)S(1)} collective-permute-done((bf16[512,1024]{1,0:T(8,128)(2,1)S(1)}, bf16[512,1024]{1,0:T(8,128)(2,1)S(1)}, u32[]{:S(2)}, u32[]{:S(2)}) %collective-permute-start.1) | collective-permute-done | bytes 1048608 | tf_op jit(solution)/shard_map/ppermute | solution.py:265
  50.7 3.5 %logits.1 = f32[512,1024]{1,0:T(8,128)S(1)} custom-call(s32[1]{0:T(128)} %bitcast.half_ref, bf16[512,1024]{1,0:T(8,128)(2,1)S(1)} %bitcast.28, bf16[512,1024]{1,0:T(8,128)(2,1)S(1)} %collective-permute-done.1.other_ref, bf16[1,1792,1024]{2,1,0:T(8,128)(2,1)S(1)} %copy-done.1, bf16[1,1792,1024]{2,1,0:T(8,128)(2,1)S(1)} %copy-done.1), custom_call_target="tpu_custom_call" | custom-call | tf_op jit(solution)/shard_map/logits/pallas_call | solution.py:32
  54.3 1.3 copy-done.4
  55.6 4.1 %all-to-all-start.1 = ((f32[4,128,1024]{2,1,0:T(8,128)}), f32[4,128,1024]{2,1,0:T(8,128)S(1)}, u32[]{:S(2)}, u32[]{:S(2)}) async-start(f32[4,128,1024]{2,1,0:T(8,128)} %bitcast.26), calls=%async_computation.1 | async-start | bytes 4194304 | tf_op jit(solution)/shard_map/all_to_all | solution.py:268
  59.9 25.6 %all-to-all-done.1.l_ref = f32[4,128,1024]{2,1,0:T(8,128)S(1)} async-done(((f32[4,128,1024]{2,1,0:T(8,128)}), f32[4,128,1024]{2,1,0:T(8,128)S(1)}, u32[]{:S(2)}, u32[]{:S(2)}) %all-to-all-start.1) | async-done | bytes 2097184 | tf_op jit(solution)/shard_map/all_to_all | solution.py:268
  85.5 2.4 %local_stats.1 = f32[8,4,8,128]{3,2,1,0:T(8,128)S(1)} custom-call(s32[4]{0:T(128)S(1)} %copy-done.5, s32[128,1]{1,0:T(8,128)S(1)} %fusion.2.tgt_ref, f32[4,128,1024]{2,1,0:T(8,128)S(1)} %all-to-all-done.1.l_ref), custom_call_target="tpu_custom_call" | custom-call | tf_op jit(solution)/shard_map/local_stats/pallas_call | solution.py:83
  87.9 9.1 %all_to_all.41.in_ref = f32[8,4,8,128]{3,2,1,0:T(8,128)S(1)} all-to-all(f32[8,4,8,128]{3,2,1,0:T(8,128)S(1)} %local_stats.1), channel_id=1, replica_groups=mesh['x'=4,'zl'=8,'c'=2,'zh'=2,'y'=4] {'c','y'}, dimensions={0} | all-to-all | bytes 262144 | tf_op jit(solution)/shard_map/all_to_all | solution.py:273
  97.2 22.8 %all_to_all.42.parts_ref = f32[16,4,8,128]{3,2,1,0:T(8,128)S(1)} all-to-all(f32[16,4,8,128]{3,2,1,0:T(8,128)S(1)} %merge_stats.1), channel_id=1, replica_groups=mesh['x'=4,'zl'=8,'c'=2,'zh'=2,'y'=4] {'zh','zl'}, dimensions={0} | all-to-all | bytes 524288 | tf_op jit(solution)/shard_map/all_to_all | solution.py:274
  120.0 5.2 %logit_grads.1 = bf16[4,144,1024]{2,1,0:T(8,128)(2,1)} custom-call(s32[4]{0:T(128)S(1)} %copy-done.5, f32[16,4,8,128]{3,2,1,0:T(8,128)S(1)} %all_to_all.42.parts_ref, s32[128,1]{1,0:T(8,128)S(1)} %fusion.2.tgt_ref, f32[4,128,1024]{2,1,0:T(8,128)S(1)} %all-to-all-done.1.l_ref), custom_call_target="tpu_custom_call" | custom-call | tf_op jit(solution)/shard_map/logit_grads/pallas_call | solution.py:192
  125.2 3.5 %all-to-all-start.4 = ((bf16[4,144,1024]{2,1,0:T(8,128)(2,1)}), bf16[4,144,1024]{2,1,0:T(8,128)(2,1)S(1)}, u32[]{:S(2)}, u32[]{:S(2)}) async-start(bf16[4,144,1024]{2,1,0:T(8,128)(2,1)} %logit_grads.1), calls=%async_computation.4 | async-start | bytes 2359296 | tf_op jit(solution)/shard_map/all_to_all | solution.py:275
  128.8 10.9 %all-to-all-done.4.g_ref = bf16[4,144,1024]{2,1,0:T(8,128)(2,1)S(1)} async-done(((bf16[4,144,1024]{2,1,0:T(8,128)(2,1)}), bf16[4,144,1024]{2,1,0:T(8,128)(2,1)S(1)}, u32[]{:S(2)}, u32[]{:S(2)}) %all-to-all-start.4) | async-done | bytes 1179680 | tf_op jit(solution)/shard_map/all_to_all | solution.py:275
  139.7 2.0 copy-done.2
  141.7 3.2 %head_grads.3 = bf16[512,896]{1,0:T(8,128)(2,1)S(1)} custom-call(s32[1]{0:T(128)S(6)} %sub.11.half_ref, bf16[4,144,1024]{2,1,0:T(8,128)(2,1)S(1)} %all-to-all-done.4.g_ref, bf16[1,1792,1024]{2,1,0:T(8,128)(2,1)S(1)} %copy-done.2), custom_call_target="tpu_custom_call" | custom-call | tf_op jit(solution)/shard_map/head_grads/pallas_call | solution.py:227
  144.9 8.4 %collective-permute-start.2 = (bf16[512,896]{1,0:T(8,128)(2,1)S(1)}, bf16[512,896]{1,0:T(8,128)(2,1)S(1)}, u32[]{:S(2)}, u32[]{:S(2)}) collective-permute-start(bf16[512,896]{1,0:T(8,128)(2,1)S(1)} %head_grads.3), channel_id=1, source_target_pairs={{0,8},{8,0},{1,9},{9,1},{2,10},{10,2},{3,11},{11,3},{4,12},{12,4},... | collective-permute-start | bytes 2752520 | tf_op jit(solution)/shard_map/ppermute | solution.py:280
  153.3 3.2 %head_grads.2 = f32[512,896]{1,0:T(8,128)S(1)} custom-call(s32[1]{0:T(128)} %bitcast.half_ref, bf16[4,144,1024]{2,1,0:T(8,128)(2,1)S(1)} %all-to-all-done.4.g_ref, bf16[1,1792,1024]{2,1,0:T(8,128)(2,1)S(1)} %copy-done.3), custom_call_target="tpu_custom_call" | custom-call | tf_op jit(solution)/shard_map/head_grads/pallas_call | solution.py:227
  156.7 16.0 %all_to_all.43 = bf16[4,128,896]{2,1,0:T(8,128)(2,1)S(1)} all-to-all(bf16[4,128,896]{2,1,0:T(8,128)(2,1)S(1)} %bitcast.30), channel_id=1, replica_groups=mesh['x'=4,'zl'=8,'c'=2,'zh'=2,'y'=4] {'y'}, dimensions={0} | all-to-all | bytes 1835008 | tf_op jit(solution)/shard_map/all_to_all | solution.py:283
  173.5 10.3 %all-to-all-start.6 = ((bf16[16,8,896]{2,1,0:T(8,128)(2,1)}), bf16[16,8,896]{2,1,0:T(8,128)(2,1)S(1)}, u32[]{:S(2)}, u32[]{:S(2)}) async-start(bf16[16,8,896]{2,1,0:T(8,128)(2,1)} %bitcast.11), calls=%async_computation.6 | async-start | bytes 458752 | tf_op jit(solution)/shard_map/all_to_all | solution.py:285
  184.0 12.5 %all-to-all-done.6 = bf16[16,8,896]{2,1,0:T(8,128)(2,1)S(1)} async-done(((bf16[16,8,896]{2,1,0:T(8,128)(2,1)}), bf16[16,8,896]{2,1,0:T(8,128)(2,1)S(1)}, u32[]{:S(2)}, u32[]{:S(2)}) %all-to-all-start.6) | async-done | bytes 229408 | tf_op jit(solution)/shard_map/all_to_all | solution.py:285
  197.3 11.0 %all-to-all-start.7 = ((bf16[16,8,896]{2,1,0:T(8,128)(2,1)}), bf16[16,8,896]{2,1,0:T(8,128)(2,1)S(1)}, u32[]{:S(2)}, u32[]{:S(2)}) async-start(bf16[16,8,896]{2,1,0:T(8,128)(2,1)} %broadcast_in_dim.5), calls=%async_computation.7 | async-start | bytes 458752 | tf_op jit(solution)/shard_map/all_to_all | solution.py:288
  208.9 15.2 %all-to-all-done.7 = bf16[16,8,896]{2,1,0:T(8,128)(2,1)S(1)} async-done(((bf16[16,8,896]{2,1,0:T(8,128)(2,1)}), bf16[16,8,896]{2,1,0:T(8,128)(2,1)S(1)}, u32[]{:S(2)}, u32[]{:S(2)}) %all-to-all-start.7) | async-done | bytes 229408 | tf_op jit(solution)/shard_map/all_to_all | solution.py:288
  (32 shorter events, 4.7 us)
Async XLA Ops:
  0.6 1.0 copy-start
  1.6 24.4 %collective-permute-start = (bf16[64,1024]{1,0:T(8,128)(2,1)S(1)}, bf16[64,1024]{1,0:T(8,128)(2,1)S(1)}, u32[]{:S(2)}, u32[]{:S(2)}) collective-permute-start(bf16[64,1024]{1,0:T(8,128)(2,1)S(1)} %get-tuple-element.3), channel_id=1, source_target_pairs={{0,68},{16,84},{32,100},{48,116},{64,4},{80,20},{96,36},{112,52},{... | collective-permute-start | bytes 393224 | tf_op jit(solution)/shard_map/ppermute | solution.py:260
  26.1 24.6 %copy-start.1 = (bf16[1,1792,1024]{2,1,0:T(8,128)(2,1)S(1)}, bf16[1,1792,1024]{2,1,0:T(8,128)(2,1)}, u32[]{:S(2)}) copy-start(bf16[1,1792,1024]{2,1,0:T(8,128)(2,1)} %w_ref.3) | copy-start | bytes 11010052
  44.1 6.6 %collective-permute-start.1 = (bf16[512,1024]{1,0:T(8,128)(2,1)S(1)}, bf16[512,1024]{1,0:T(8,128)(2,1)S(1)}, u32[]{:S(2)}, u32[]{:S(2)}) collective-permute-start(bf16[512,1024]{1,0:T(8,128)(2,1)S(1)} %bitcast.27), channel_id=1, source_target_pairs={{0,8},{8,0},{1,9},{9,1},{2,10},{10,2},{3,11},{11,3},{4,12},{12,4},... | collective-permute-start | bytes 3145736 | tf_op jit(solution)/shard_map/ppermute | solution.py:265
  54.2 1.3 copy-start.4
  55.6 29.9 %copy-start.5 = (s32[4]{0:T(128)S(1)}, s32[4]{0:T(128)}, u32[]{:S(2)}) copy-start(s32[4]{0:T(128)} %pair_ref.3) | copy-start | bytes 52
  55.6 29.9 %all-to-all-start.1 = ((f32[4,128,1024]{2,1,0:T(8,128)}), f32[4,128,1024]{2,1,0:T(8,128)S(1)}, u32[]{:S(2)}, u32[]{:S(2)}) async-start(f32[4,128,1024]{2,1,0:T(8,128)} %bitcast.26), calls=%async_computation.1 | async-start | bytes 4194304 | tf_op jit(solution)/shard_map/all_to_all | solution.py:268
  125.2 14.4 %all-to-all-start.4 = ((bf16[4,144,1024]{2,1,0:T(8,128)(2,1)}), bf16[4,144,1024]{2,1,0:T(8,128)(2,1)S(1)}, u32[]{:S(2)}, u32[]{:S(2)}) async-start(bf16[4,144,1024]{2,1,0:T(8,128)(2,1)} %logit_grads.1), calls=%async_computation.4 | async-start | bytes 2359296 | tf_op jit(solution)/shard_map/all_to_all | solution.py:275
  139.7 2.0 copy-start.2
  141.7 11.6 %copy-start.3 = (bf16[1,1792,1024]{2,1,0:T(8,128)(2,1)S(1)}, bf16[1,1792,1024]{2,1,0:T(8,128)(2,1)}, u32[]{:S(2)}) copy-start(bf16[1,1792,1024]{2,1,0:T(8,128)(2,1)} %w_ref.3) | copy-start | bytes 11010052
  144.9 11.6 %collective-permute-start.2 = (bf16[512,896]{1,0:T(8,128)(2,1)S(1)}, bf16[512,896]{1,0:T(8,128)(2,1)S(1)}, u32[]{:S(2)}, u32[]{:S(2)}) collective-permute-start(bf16[512,896]{1,0:T(8,128)(2,1)S(1)} %head_grads.3), channel_id=1, source_target_pairs={{0,8},{8,0},{1,9},{9,1},{2,10},{10,2},{3,11},{11,3},{4,12},{12,4},... | collective-permute-start | bytes 2752520 | tf_op jit(solution)/shard_map/ppermute | solution.py:280
  156.7 27.2 %copy-start.6 = (f32[1,64]{1,0:T(1,128)S(1)}, f32[1,64]{1,0:T(1,128)}, u32[]{:S(2)}) copy-start(f32[1,64]{1,0:T(1,128)} %param.9) | copy-start | bytes 772
  173.5 22.9 %all-to-all-start.6 = ((bf16[16,8,896]{2,1,0:T(8,128)(2,1)}), bf16[16,8,896]{2,1,0:T(8,128)(2,1)S(1)}, u32[]{:S(2)}, u32[]{:S(2)}) async-start(bf16[16,8,896]{2,1,0:T(8,128)(2,1)} %bitcast.11), calls=%async_computation.6 | async-start | bytes 458752 | tf_op jit(solution)/shard_map/all_to_all | solution.py:285
  197.3 26.8 %all-to-all-start.7 = ((bf16[16,8,896]{2,1,0:T(8,128)(2,1)}), bf16[16,8,896]{2,1,0:T(8,128)(2,1)S(1)}, u32[]{:S(2)}, u32[]{:S(2)}) async-start(bf16[16,8,896]{2,1,0:T(8,128)(2,1)} %broadcast_in_dim.5), calls=%async_computation.7 | async-start | bytes 458752 | tf_op jit(solution)/shard_map/all_to_all | solution.py:288

commit v2 on v0

v2 whole, which is shorter than its diff:
```python
import functools

import jax
import jax.numpy as jnp
from jax import lax
from jax.experimental import pallas as pl
from jax.experimental.pallas import tpu as pltpu
from jax.sharding import Mesh
from jax.sharding import PartitionSpec as P

kl_weight = 1.0
F32 = jnp.float32
BF16 = jnp.bfloat16
Z = ("zh", "zl")
FAR = {0: 12, 1: 13, 2: 14, 3: 15, 4: 8, 5: 9, 6: 10, 7: 11}
FAR.update({b: a for a, b in FAR.items()})
SWAP_Z = [(z % 8 * 2 + z // 8, FAR[z] % 8 * 2 + FAR[z] // 8) for z in range(16)]
SWAP_C = [(0, 1), (1, 0)]
PAIRINGS = ((2, 3, 1, 0), (3, 2, 0, 1), (1, 3, 0, 2), (2, 0, 3, 1))
LANES = 128
TILE = 32


def call(kernel, outs, operands, name, scratch=(), flops=0):
    scalars = [o.ndim == 1 for o in operands]
    vmem, smem = pl.BlockSpec(memory_space=pltpu.VMEM), pl.BlockSpec(memory_space=pltpu.SMEM)
    moved = sum(o.size * o.dtype.itemsize for o in list(operands) + list(outs))
    return pl.pallas_call(
        kernel,
        out_shape=outs if len(outs) > 1 else outs[0],
        in_specs=[smem if s else vmem for s in scalars],
        out_specs=[vmem] * len(outs) if len(outs) > 1 else vmem,
        scratch_shapes=scratch,
        compiler_params=pltpu.CompilerParams(vmem_limit_bytes=moved + (6 << 20)),
        cost_estimate=pl.CostEstimate(flops=flops, bytes_accessed=moved, transcendentals=0),
        name=name,
    )(*operands)


def shape(*dims, dtype=F32):
    return jax.ShapeDtypeStruct(dims, dtype)


def tiles(rows, step=TILE):
    def run(body):
        def at(i, carry):
            body(pl.ds(pl.multiple_of(i * step, step), step))
            return carry

        lax.fori_loop(0, rows // step, at, 0)

    return run


def packed(values, rows):
    lane = lax.broadcasted_iota(jnp.int32, (rows, LANES), 1)
    out = jnp.zeros((rows, LANES), F32)
    for i, v in enumerate(values):
        if v is not None:
            out = jnp.where(lane == i, v, out)
    return out


def forward_kernel(h_ref, w_ref, x_ref, sent_ref, top_ref):
    width = w_ref.shape[2]
    at = pl.ds(pl.multiple_of(pl.program_id(0) * width, width), width)
    x_ref[:, at] = jnp.dot(h_ref[...], w_ref[0], preferred_element_type=F32)

    @pl.when(pl.program_id(0) == pl.num_programs(0) - 1)
    def _():
        below_top(x_ref, sent_ref, top_ref)


def below_top(x_ref, sent_ref, top_ref):
    rows, vocab = x_ref.shape

    @tiles(rows)
    def _(at):
        logits = x_ref[at]
        top = jnp.max(logits, axis=1, keepdims=True)
        below = logits - top
        x_ref[at] = below
        square = below * below
        sent_ref[at] = (square * square).astype(BF16)
        top_ref[at] = jnp.broadcast_to(top, (TILE, LANES))

    row = lax.broadcasted_iota(jnp.int32, (16, LANES), 0)
    sent_ref[rows:] = jnp.zeros((16, vocab), BF16)
    for b in range(rows // LANES):
        top = jnp.transpose(top_ref[b * LANES : (b + 1) * LANES])[:16]
        high = top.astype(BF16).astype(F32)
        middle = (top - high).astype(BF16).astype(F32)
        low = (top - high) - middle
        pieces = jnp.where(row == 0, high, jnp.where(row == 1, middle, low))
        pieces = jnp.where(row < 3, pieces, 0.0)
        sent_ref[rows:, b * LANES : (b + 1) * LANES] = pieces.astype(BF16)


def forward(h, head):
    rows, features, vocab = h.shape[0], h.shape[1], head.shape[2]
    width = 256
    outs = [shape(rows, vocab), shape(rows + 16, vocab, dtype=BF16), shape(rows, LANES)]
    return pl.pallas_call(
        forward_kernel,
        out_shape=outs,
        grid=(vocab // width,),
        in_specs=[
            pl.BlockSpec(h.shape, lambda n: (0, 0)),
            pl.BlockSpec((1, features, width), lambda n: (0, 0, n)),
        ],
        out_specs=[pl.BlockSpec(o.shape, lambda n: (0, 0)) for o in outs],
        compiler_params=pltpu.CompilerParams(vmem_limit_bytes=16 << 20),
        cost_estimate=pl.CostEstimate(
            flops=2 * rows * features * vocab, bytes_accessed=6 << 20, transcendentals=0
        ),
        name="logits",
    )(h, head)


def target_column(ids_ref, at, offset):
    ids = ids_ref[at].astype(jnp.int32)
    lane = lax.broadcasted_iota(jnp.int32, ids.shape, 1)
    ids = jnp.where(lane == 0, ids * 4096, jnp.where(lane == 1, ids * 64, ids))
    return jnp.sum(ids.astype(F32), axis=1, keepdims=True).astype(jnp.int32) - offset


def own_kernel(offset_ref, ids_ref, x_ref, top_ref, power_ref, cols_ref):
    rows, vocab = x_ref.shape
    column = lax.broadcasted_iota(jnp.int32, (TILE, vocab), 1)

    @tiles(rows)
    def _(at):
        below = x_ref[at]
        top = top_ref[at, 0:1]
        power = jnp.exp(below)
        power_ref[at] = power
        hit = column == target_column(ids_ref, at, offset_ref[0])
        mine = jnp.sum(jnp.where(hit, below + top, 0.0), axis=1, keepdims=True)
        total = jnp.sum(power, axis=1, keepdims=True)
        cols_ref[at] = packed((top, total, None, mine), TILE)


def peer_half(x_ref, power_ref, cols_ref, got_ref, all_ref):
    rows = x_ref.shape[0]

    @tiles(rows)
    def _(at):
        below = -jnp.sqrt(jnp.sqrt(got_ref[at].astype(F32)))
        gap = x_ref[at] - below
        peer = jnp.exp(below)
        to_peer = jnp.sum(power_ref[at] * gap, axis=1, keepdims=True)
        total = jnp.sum(peer, axis=1, keepdims=True)
        to_own = -jnp.sum(peer * gap, axis=1, keepdims=True)
        all_ref[at] = cols_ref[at] + packed((None, None, to_peer, None, None, total, to_own), TILE)

    parts = []
    for b in range(rows // LANES):
        lanes = slice(b * LANES, (b + 1) * LANES)
        flat = jnp.transpose(all_ref[lanes])
        top, total = flat[0:1], flat[1:2]
        high, middle, low = (got_ref[rows : rows + 16, lanes].astype(F32)[i : i + 1] for i in range(3))
        peer_top = high + (middle + low)
        step = top - peer_top
        row = lax.broadcasted_iota(jnp.int32, (8, LANES), 0)
        out = flat[:8]
        out = jnp.where(row == 2, out + total * step, out)
        out = jnp.where(row == 4, peer_top, out)
        parts.append(jnp.where(row == 6, out - flat[5:6] * step, out))
    return jnp.concatenate(parts, axis=1)


def stats_near_kernel(x_ref, power_ref, cols_ref, got_ref, out_ref, all_ref):
    out_ref[...] = peer_half(x_ref, power_ref, cols_ref, got_ref, all_ref)


def stats_far_kernel(zh_ref, near_ref, x_ref, power_ref, cols_ref, got_ref, out_ref, all_ref):
    rows = x_ref.shape[0]
    far = peer_half(x_ref, power_ref, cols_ref, got_ref, all_ref)
    near_at = pl.ds(pl.multiple_of(zh_ref[0] * rows, rows), rows)
    far_at = pl.ds(pl.multiple_of((1 - zh_ref[0]) * rows, rows), rows)
    near = near_ref[...]
    for k in range(out_ref.shape[0]):
        out_ref[k, :, near_at] = near
        out_ref[k, :, far_at] = far


def merged(parts):
    out = []
    for first in (0, 4):
        top = jnp.max(parts[:, first], axis=0, keepdims=True)
        scale = jnp.exp(parts[:, first] - top)
        total = jnp.sum(parts[:, first + 1] * scale, axis=0, keepdims=True)
        mixed = jnp.sum(parts[:, first + 2] * scale, axis=0, keepdims=True)
        out += [top, total, mixed]
    return out[:3] + [jnp.sum(parts[:, 3], axis=0, keepdims=True)] + out[3:]


def merge_kernel(core_ref, in_ref, out_ref):
    count = out_ref.shape[2]
    values = merged(in_ref[:, :, pl.ds(pl.multiple_of(core_ref[0] * count, count), count)])
    values = jnp.concatenate(values + [jnp.zeros_like(values[0])], axis=0)
    for k in range(out_ref.shape[0]):
        out_ref[k] = values


def last_merge_kernel(in_ref, out_ref):
    values = merged(in_ref[...])
    out_ref[...] = jnp.concatenate(values + [jnp.zeros_like(values[0])], axis=0)


def grad_kernel(
    where_ref, whole_ref, local_ref, ids_ref, x_near, x_far, got_near, got_far,
    out_ref, loss_ref, flat_ref, cols_ref,
):
    step_at = pl.program_id(0)
    rows, vocab = out_ref.shape
    half = whole_ref.shape[2]

    @pl.when(step_at == 0)
    def _():
        flat_ref[...] = jnp.zeros_like(flat_ref)
        loss_ref[...] = jnp.zeros_like(loss_ref)
        for i in range(2):
            zh = where_ref[0] if i == 0 else 1 - where_ref[0]
            lanes = pl.ds(pl.multiple_of(zh * half, half), half)
            top, total, to_peer, target, peer_top, peer_total, to_own = (
                whole_ref[zh, k : k + 1, :] for k in range(7)
            )
            log_total = top + jnp.log(total)
            peer_log_total = peer_top + jnp.log(peer_total)
            step = log_total - peer_log_total
            reverse = to_peer / total - step
            forward_kl = to_own / peer_total + step
            loss_ref[0:1, lanes] = log_total - target + 0.5 * kl_weight * (forward_kl + reverse)
            own_top, own_peer_top = local_ref[0, 0:1, lanes], local_ref[0, 4:5, lanes]
            flat_ref[0:1] = jnp.exp(own_top - log_total)
            flat_ref[1:2] = (0.5 * kl_weight) * jnp.exp(own_peer_top - peer_log_total)
            flat_ref[2:3] = (1.0 + 0.5 * kl_weight) + 0.5 * kl_weight * (
                (own_top - own_peer_top) - step - reverse
            )
            for b in range(half // LANES):
                to = i * half + b * LANES
                cols_ref[to : to + LANES] = jnp.transpose(flat_ref[:, b * LANES : (b + 1) * LANES])

    def block(x_ref, got_ref):
        column = lax.broadcasted_iota(jnp.int32, (16, vocab), 1)

        @tiles(rows, 16)
        def _(at):
            here = pl.ds(pl.multiple_of(step_at * rows + at.start, 16), 16)
            below = x_ref[at]
            peer_below = -jnp.sqrt(jnp.sqrt(got_ref[at].astype(F32)))
            hit = column == target_column(ids_ref, at, where_ref[1])
            own_prob = jnp.exp(below) * cols_ref[here, 0:1]
            gap = below - peer_below
            inner = own_prob * (cols_ref[here, 2:3] + (0.5 * kl_weight) * gap)
            inner = inner - jnp.exp(peer_below) * cols_ref[here, 1:2] - jnp.where(hit, 1.0, 0.0)
            out_ref[at] = inner.astype(BF16)

    pl.when(step_at < 4)(lambda: block(x_near, got_near))
    pl.when(step_at >= 4)(lambda: block(x_far, got_far))


def logit_grads(where, whole, local, ids, x_near, x_far, got_near, got_far):
    half, vocab = x_near.shape
    rows = half // 4
    near = pl.BlockSpec((rows, vocab), lambda n, w: (jnp.minimum(n, 3), 0))
    far = pl.BlockSpec((rows, vocab), lambda n, w: (jnp.maximum(n - 4, 0), 0))

    def place(n, w):
        return (2 * (n % 4) + jnp.where(n < 4, w[0], 1 - w[0]), 0)

    return pl.pallas_call(
        grad_kernel,
        out_shape=[shape(2 * half, vocab, dtype=BF16), shape(8, 2 * half)],
        grid_spec=pltpu.PrefetchScalarGridSpec(
            num_scalar_prefetch=1,
            grid=(8,),
            in_specs=[
                pl.BlockSpec(whole.shape, lambda n, w: (0, 0, 0)),
                pl.BlockSpec(local.shape, lambda n, w: (0, 0, 0)),
                pl.BlockSpec((rows, LANES), lambda n, w: (n, 0)),
                near,
                far,
                near,
                far,
            ],
            out_specs=[
                pl.BlockSpec((rows, vocab), place),
                pl.BlockSpec((8, 2 * half), lambda n, w: (0, 0)),
            ],
            scratch_shapes=[pltpu.VMEM((LANES, half), F32), pltpu.VMEM((2 * half, LANES), F32)],
        ),
        compiler_params=pltpu.CompilerParams(vmem_limit_bytes=16 << 20),
        cost_estimate=pl.CostEstimate(flops=1, bytes_accessed=4 << 20, transcendentals=0),
        name="logit_grads",
    )(where, whole, local, ids, x_near, x_far, got_near, got_far)


def backward_kernel(half_ref, g_ref, w_ref, out_ref):
    depth = out_ref.shape[1]
    first = half_ref[0] * depth
    for n in range(0, depth, 256):
        width = min(256, depth - n)
        rows = w_ref[0, pl.ds(pl.multiple_of(first + n, LANES), width), :]
        out_ref[:, n : n + width] = lax.dot_general(
            g_ref[...], rows, (((1,), (1,)), ((), ())), preferred_element_type=F32
        ).astype(out_ref.dtype)


def backward(half, grads, head, dtype):
    rows, depth = grads.shape[0], head.shape[1] // 2
    return call(
        backward_kernel,
        [shape(rows, depth, dtype=dtype)],
        (half, grads, head),
        "head_grads",
        flops=2 * rows * depth * head.shape[2],
    )


def spread(block):
    out = lax.all_to_all(jnp.broadcast_to(block[None], (4,) + block.shape), "y", 0, 0)
    return out.reshape(-1, block.shape[1])


def logits_of(block, head):
    h = lax.all_gather(block[:, : head.shape[1] // 2], "c", axis=1, tiled=True)
    return forward(h, head)


def own_of(offset, ids, x, top):
    outs = [shape(*x.shape), shape(x.shape[0], LANES)]
    return call(own_kernel, outs, (offset, ids, x, top), "own_stats")


def exchange(partner, near, far, head, where):
    to_learner = [(partner[r], r) for r in range(4)]
    near_ids, x_near, sent, top_near = near
    offset = where[1:2]
    half = x_near.shape[0]
    depth = head.shape[1] // 2
    got_near = lax.ppermute(sent, "x", to_learner)
    far_h = spread(far)
    far_ids = far_h[:, depth:]
    x_far, sent, top_far = logits_of(far_h, head)
    sent, x_near = lax.optimization_barrier((sent, x_near))
    got_far = lax.ppermute(sent, "x", to_learner)
    power_near, cols_near = own_of(offset, near_ids, x_near, top_near)
    power_far, cols_far = own_of(offset, far_ids, x_far, top_far)
    scratch = [pltpu.VMEM((half, LANES), F32)]
    near = call(
        stats_near_kernel,
        [shape(8, half)],
        (x_near, power_near, cols_near, got_near),
        "near_stats",
        scratch,
    )
    local = call(
        stats_far_kernel,
        [shape(8, 8, 2 * half)],
        (where, near, x_far, power_far, cols_far, got_far),
        "far_stats",
        scratch,
    )
    return local, far_ids, x_far, got_near, got_far


def on_device(hidden, head_weight, targets, pairing, token_weight):
    zl, c, zh, y = (lax.axis_index(a) for a in ("zl", "c", "zh", "y"))
    rows, features = hidden.shape[1], hidden.shape[2]
    depth = features // 2
    vocab = head_weight.shape[2]
    offset = (((zl * 2 + c) * 2 + zh) * 4 + y) * vocab
    half = 4 * rows
    core = c.reshape(1)
    where = jnp.stack([zh, offset])

    ids = jnp.stack([targets >> 12, (targets >> 6) & 63, targets & 63], axis=1).astype(BF16)
    mine = jnp.concatenate(
        [
            lax.dynamic_slice_in_dim(hidden[0], c * depth, depth, 1),
            jnp.pad(ids, ((0, 0), (0, LANES - 3))),
        ],
        axis=1,
    )
    far = lax.ppermute(mine, ("zl", "zh"), SWAP_Z)
    near_h = spread(mine)
    near_ids = near_h[:, depth:]
    x_near, sent, top_near = logits_of(near_h, head_weight)
    x_near, far = lax.optimization_barrier((x_near, far))
    first, second = pairing[0], pairing[1]
    which = jnp.where(first == 2, jnp.where(second == 3, 0, 3), jnp.where(first == 3, 1, 2))
    local, far_ids, x_far, got_near, got_far = lax.switch(
        which,
        [functools.partial(exchange, p) for p in PAIRINGS],
        (near_ids, x_near, sent, top_near), far, head_weight, where,
    )

    parts = lax.all_to_all(local, ("c", "y"), 0, 0)
    parts = call(merge_kernel, [shape(16, 8, half)], (core, parts), "merge_near")
    parts = lax.all_to_all(parts, Z, 0, 0)
    parts = call(last_merge_kernel, [shape(8, half)], (parts,), "merge_all")
    whole = lax.all_gather(parts, "c", axis=0, tiled=False)
    ids = jnp.concatenate([near_ids, far_ids], axis=0)
    grads, losses = logit_grads(where, whole, local, ids, x_near, x_far, got_near, got_far)
    loss = lax.dynamic_slice(losses, (0, zh * half + y * rows), (1, rows))
    loss = token_weight * loss

    sent = lax.ppermute(backward(1 - core, grads, head_weight, BF16), "c", SWAP_C)
    kept = backward(core, grads, head_weight, F32)
    by_y = (kept + sent.astype(F32)).astype(BF16).reshape(4, 2 * rows, depth)
    by_y = lax.all_to_all(by_y, "y", 0, 0)
    by_z = jnp.sum(by_y.astype(F32), axis=0).astype(BF16).reshape(16, rows // 8, depth)
    by_z = lax.all_to_all(by_z, Z, 0, 0)
    weights = lax.dynamic_slice_in_dim(token_weight[0], zl * (rows // 8), rows // 8, 0)
    final = (jnp.sum(by_z.astype(F32), axis=0) * weights[:, None]).astype(BF16)
    final = lax.all_to_all(jnp.broadcast_to(final[None], (8,) + final.shape), "zl", 0, 0)
    final = lax.all_gather(final.reshape(rows, depth), "c", axis=1, tiled=True)
    return (final[None], loss)


def solution(mesh):
    fine = Mesh(mesh.devices.reshape(4, 8, 2, 2, 4), ("x", "zl", "c", "zh", "y"))
    return jax.shard_map(
        on_device,
        mesh=fine,
        in_specs=(
            P("x", ("zh", "y"), None),
            P("x", None, ("zl", "c", "zh", "y")),
            P(("zh", "y")),
            P(),
            P("x", ("zh", "y")),
        ),
        out_specs=(P("x", ("zh", "y"), None), P("x", ("zh", "y"))),
        check_vma=False,
    )
```

time: 2090 us -> 184 us (0.09)
  blocking collectives: 1670 us -> 41.3 us
  waiting for transfers between devices: 375 us -> 42.4 us
  starting transfers between devices: 0.12 us -> 56 us
  Pallas kernels: 0 us -> 32.6 us
    psum x3 -> x0, blocking collectives: 1110 us -> none  [the longest x1 515 us: on_device(): lax.psum((local_total, local_target), ('vocab', 'dp'))]
    pmax x1 -> x0, blocking collectives: 507 us -> none  [on_device(): row_top = lax.pmax(local_top, ('vocab', 'dp'))]
    reduce_scatter x1 -> x0, waiting for transfers between devices: 212 us -> none  [on_device(): lax.psum_scatter(lax.dot_general(logit_grad, head_rows, (((1,), (1,)), ((...]
    all_gather x2 -> x0, waiting for transfers between devices: 162 us -> none  [the longest x1 92.9 us: on_device(): lax.all_gather(hidden, 'dp', axis=1, tiled=True)]
    unnamed x2 -> x0, blocking collectives: 53.2 us -> none
    all_to_all x0 -> x5, waiting for transfers between devices: none -> 36.6 us  [the longest x1 12.5 us: on_device(): by_z = lax.all_to_all(by_z, Z, 0, 0)]
    pallas_call x0 -> x11, Pallas kernels: none -> 32.6 us  [the longest x8 15.5 us: call(): pl.pallas_call(kernel, out_shape=outs if len(outs) > 1 else outs[0], in_s...]
    all_to_all x0 -> x5, starting transfers between devices: none -> 32.1 us  [the longest x1 9.66 us: on_device(): lax.all_to_all(jnp.broadcast_to(final[None], (8,) + final.shape), 'zl', 0...]
  transfers between devices with their start and end apart: 3 -> 9, of which waited for: 3 -> 7; matrix products, arithmetic and copies ran while one was open for 0% -> 1% of each run, Pallas kernels for 0% -> 10%
where the time goes in v2:
time: 184 us; the launch traced here: 183 us
  starting transfers between devices  56 us (30%)
  waiting for transfers between devices  42.4 us (23%)
  blocking collectives  41.3 us (22%)
  Pallas kernels  32.6 us (18%)
  local copies, waits for them, and re-layouts  4.1 us (2%)
  other arithmetic  3.38 us (2%)
  between operations  2.88 us (2%)
    all_to_all x1, blocking collectives, on_device(): by_y = lax.all_to_all(by_y, 'y', 0, 0)  15.7 us
    pallas_call x8, Pallas kernels, call(): pl.pallas_call(kernel, out_shape=outs if len(outs) > 1 else outs[0], in_s...  15.5 us
    all_to_all x1, waiting for transfers between devices, on_device(): by_z = lax.all_to_all(by_z, Z, 0, 0)  12.5 us
    ppermute x1, starting transfers between devices, on_device(): far = lax.ppermute(mine, ('zl', 'zh'), SWAP_Z)  12.4 us
    all_to_all x1, waiting for transfers between devices, on_device(): parts = lax.all_to_all(parts, Z, 0, 0)  11.3 us
    pallas_call x2, Pallas kernels, forward(): pl.pallas_call(forward_kernel, out_shape=outs, grid=(vocab // width,), in...  10.1 us
    all_to_all x1, starting transfers between devices, on_device(): lax.all_to_all(jnp.broadcast_to(final[None], (8,) + final.shape), 'zl', 0...  9.66 us
    all_to_all x1, waiting for transfers between devices, on_device(): lax.all_to_all(jnp.broadcast_to(final[None], (8,) + final.shape), 'zl', 0...  9.56 us
  transfers between devices with their start and end apart: 9, of which 7 were waited for; matrix products, arithmetic and copies ran while one was open for 1% of the time, Pallas kernels for 10%

profile of v2, /device:TPU:1, one launch (start us, length us, event | category | flops | bytes accessed | tf_op | source)
XLA Modules:
  0.0 182.8 jit_solution(17682005973374438682)
XLA Ops:
  2.5 5.0 %all-to-all-start.4 = ((bf16[4,64,1024]{2,1,0:T(8,128)(2,1)}), bf16[4,64,1024]{2,1,0:T(8,128)(2,1)S(1)}, u32[]{:S(2)}, u32[]{:S(2)}) async-start(bf16[4,64,1024]{2,1,0:T(8,128)(2,1)} %broadcast_in_dim.22), calls=%async_computation.4 | async-start | bytes 1048576 | tf_op jit(solution)/shard_map/all_to_all | solution.py:323
  7.5 12.4 %collective-permute-start.8 = (bf16[64,1024]{1,0:T(8,128)(2,1)S(1)}, bf16[64,1024]{1,0:T(8,128)(2,1)S(1)}, u32[]{:S(2)}, u32[]{:S(2)}) collective-permute-start(bf16[64,1024]{1,0:T(8,128)(2,1)S(1)} %fusion.1), channel_id=1, source_target_pairs={{0,68},{16,84},{32,100},{48,116},{64,4},{80,20},{96,36},{112,52},{... | collective-permute-start | bytes 393224 | tf_op jit(solution)/shard_map/ppermute | solution.py:387
  22.7 3.3 %all_gather.24.h_ref = bf16[256,1792]{1,0:T(8,128)(2,1)S(1)} all-gather(bf16[256,896]{1,0:T(8,128)(2,1)S(1)} %slice.48), channel_id=1, replica_groups=mesh['x'=4,'zl'=8,'c'=2,'zh'=2,'y'=4] {'c'}, dimensions={1}, use_global_device_ids=true | all-gather | bytes 1376256 | tf_op jit(solution)/shard_map/all_gather | solution.py:328
  26.1 4.5 %logits.9 = (f32[256,1024]{1,0:T(8,128)S(1)}, bf16[272,1024]{1,0:T(8,128)(2,1)S(1)}, f32[256,128]{1,0:T(8,128)S(1)}) custom-call(bf16[256,1792]{1,0:T(8,128)(2,1)S(1)} %all_gather.24.h_ref, bf16[1,1792,1024]{2,1,0:T(8,128)(2,1)} %w_ref.5), custom_call_target="tpu_custom_call" | custom-call | flops 939524096 | bytes 6291456 | tf_op jit(solution)/shard_map/logits/pallas_call | solution.py:103
  31.1 42.4 %conditional.1 = (f32[8,8,512]{2,1,0:T(8,128)S(1)}, bf16[256,128]{1,0:T(8,128)(2,1)}, f32[256,1024]{1,0:T(8,128)}, bf16[272,1024]{1,0:T(8,128)(2,1)}, bf16[272,1024]{1,0:T(8,128)(2,1)}) conditional(s32[]{:T(128)} %bitcast.7, (bf16[64,1024]{1,0:T(8,128)(2,1)S(1)}, bf16[1,1792,1024]{2,1,0:T(8,128)(2,1)}, ...), branch_computations={%region_0.1_spmd, %region_1.2_spmd, %region_2.3_spmd, %region_3.4_... | conditional | flops 939524096 | bytes 26230980 | solution.py:394
  31.9 4.2 %all-to-all-start.2 = ((bf16[4,64,1024]{2,1,0:T(8,128)(2,1)}), bf16[4,64,1024]{2,1,0:T(8,128)(2,1)S(1)}, u32[]{:S(2)}, u32[]{:S(2)}) async-start(bf16[4,64,1024]{2,1,0:T(8,128)(2,1)} %broadcast_in_dim.7), calls=%async_computation.2 | async-start | bytes 1048576 | tf_op jit(solution)/shard_map/cond/branch_2_fun/all_to_all | solution.py:323
  36.2 4.6 %collective-permute-start.4 = (bf16[272,1024]{1,0:T(8,128)(2,1)S(1)}, bf16[272,1024]{1,0:T(8,128)(2,1)}, u32[]{:S(2)}, u32[]{:S(2)}) collective-permute-start(bf16[272,1024]{1,0:T(8,128)(2,1)S(1)} %get-tuple-element.109), channel_id=1, source_target_pairs={{128,0},{384,128},{0,256},{256,384},{129,1},{385,129},{1,257},{257... | collective-permute-start | bytes 1671176 | tf_op jit(solution)/shard_map/cond/branch_2_fun/ppermute | solution.py:343
  40.8 3.3 %all-to-all-done.2 = bf16[4,64,1024]{2,1,0:T(8,128)(2,1)S(1)} async-done(((bf16[4,64,1024]{2,1,0:T(8,128)(2,1)}), bf16[4,64,1024]{2,1,0:T(8,128)(2,1)S(1)}, u32[]{:S(2)}, u32[]{:S(2)}) %all-to-all-start.2) | async-done | bytes 524320 | tf_op jit(solution)/shard_map/cond/branch_2_fun/all_to_all | solution.py:323
  44.1 4.6 %all_gather.18.h_ref = bf16[256,1792]{1,0:T(8,128)(2,1)S(1)} all-gather(bf16[256,896]{1,0:T(8,128)(2,1)S(1)} %slice.44), channel_id=1, replica_groups=mesh['x'=4,'zl'=8,'c'=2,'zh'=2,'y'=4] {'c'}, dimensions={1}, use_global_device_ids=true | all-gather | bytes 1376256 | tf_op jit(solution)/shard_map/cond/branch_2_fun/all_gather | solution.py:328
  48.7 5.6 %logits.7 = (f32[256,1024]{1,0:T(8,128)}, bf16[272,1024]{1,0:T(8,128)(2,1)S(1)}, f32[256,128]{1,0:T(8,128)S(1)}) custom-call(bf16[256,1792]{1,0:T(8,128)(2,1)S(1)} %all_gather.18.h_ref, bf16[1,1792,1024]{2,1,0:T(8,128)(2,1)} %get-tuple-element.100.w_ref), custom_call_target="tpu_custom_call" | custom-call | flops 939524096 | bytes 6291456 | tf_op jit(solution)/shard_map/cond/branch_2_fun/logits/pallas_call | solution.py:103
  54.3 4.6 %collective-permute-start.5 = (bf16[272,1024]{1,0:T(8,128)(2,1)S(1)}, bf16[272,1024]{1,0:T(8,128)(2,1)}, u32[]{:S(2)}, u32[]{:S(2)}) collective-permute-start(bf16[272,1024]{1,0:T(8,128)(2,1)S(1)} %get-tuple-element.114), channel_id=1, source_target_pairs={{128,0},{384,128},{0,256},{256,384},{129,1},{385,129},{1,257},{257... | collective-permute-start | bytes 1671176 | tf_op jit(solution)/shard_map/cond/branch_2_fun/ppermute | solution.py:348
  66.0 4.6 %collective-permute-done.5.got_ref = bf16[272,1024]{1,0:T(8,128)(2,1)} collective-permute-done((bf16[272,1024]{1,0:T(8,128)(2,1)S(1)}, bf16[272,1024]{1,0:T(8,128)(2,1)}, u32[]{:S(2)}, u32[]{:S(2)}) %collective-permute-start.5) | collective-permute-done | bytes 557088 | tf_op jit(solution)/shard_map/cond/branch_2_fun/ppermute | solution.py:348
  73.5 8.7 %all_to_all.46.in_ref = f32[8,8,512]{2,1,0:T(8,128)S(1)} all-to-all(f32[8,8,512]{2,1,0:T(8,128)S(1)} %get-tuple-element.151.local_ref), channel_id=1, replica_groups=mesh['x'=4,'zl'=8,'c'=2,'zh'=2,'y'=4] {'c','y'}, dimensions={0} | all-to-all | bytes 262144 | tf_op jit(solution)/shard_map/all_to_all | solution.py:400
  83.0 9.2 %all-to-all-start.6 = ((f32[16,8,256]{2,1,0:T(8,128)}), f32[16,8,256]{2,1,0:T(8,128)S(1)}, u32[]{:S(2)}, u32[]{:S(2)}) async-start(f32[16,8,256]{2,1,0:T(8,128)} %merge_near.1), calls=%async_computation.6 | async-start | bytes 262144 | tf_op jit(solution)/shard_map/all_to_all | solution.py:402
  93.0 11.3 %all-to-all-done.6.in_ref = f32[16,8,256]{2,1,0:T(8,128)S(1)} async-done(((f32[16,8,256]{2,1,0:T(8,128)}), f32[16,8,256]{2,1,0:T(8,128)S(1)}, u32[]{:S(2)}, u32[]{:S(2)}) %all-to-all-start.6) | async-done | bytes 131104 | tf_op jit(solution)/shard_map/all_to_all | solution.py:402
  104.4 4.7 %all-gather = f32[16,256]{1,0:T(8,128)S(1)} all-gather(f32[8,256]{1,0:T(8,128)S(1)} %merge_all.1), channel_id=2, replica_groups=mesh['x'=4,'zl'=8,'c'=2,'zh'=2,'y'=4] {'c'}, dimensions={0}, use_global_device_ids=true | all-gather | bytes 24576 | tf_op jit(solution)/shard_map/all_gather | solution.py:404
  109.1 7.0 %logit_grads.1 = (bf16[512,1024]{1,0:T(8,128)(2,1)S(1)}, f32[8,512]{1,0:T(8,128)S(1)}) custom-call(s32[2]{0:T(128)S(1)} %pad_add_fusion.where_ref, f32[2,8,256]{2,1,0:T(8,128)S(1)} %bitcast.24, f32[8,8,512]{2,1,0:T(8,128)S(1)} %get-tuple-element.151.local_ref, bf16[512,128]{1,0:T(8,128)(2,1)S(1)} %pad_maximum_fusion.ids_ref, ...), custom_call_target="tpu_custom_call" | custom-call | flops 1 | bytes 4194304 | tf_op jit(solution)/shard_map/logit_grads/pallas_call | solution.py:273
  116.1 3.5 %head_grads.3 = bf16[512,896]{1,0:T(8,128)(2,1)S(1)} custom-call(s32[1]{0:T(128)S(6)} %sub.3.half_ref, bf16[512,1024]{1,0:T(8,128)(2,1)S(1)} %get-tuple-element.156.g_ref, bf16[1,1792,1024]{2,1,0:T(8,128)(2,1)} %w_ref.5), custom_call_target="tpu_custom_call" | custom-call | flops 939524096 | bytes 5636100 | tf_op jit(solution)/shard_map/head_grads/pallas_call | solution.py:28
  124.1 15.7 %all_to_all.47 = bf16[4,128,896]{2,1,0:T(8,128)(2,1)S(1)} all-to-all(bf16[4,128,896]{2,1,0:T(8,128)(2,1)S(1)} %bitcast.25), channel_id=1, replica_groups=mesh['x'=4,'zl'=8,'c'=2,'zh'=2,'y'=4] {'y'}, dimensions={0} | all-to-all | bytes 1835008 | tf_op jit(solution)/shard_map/all_to_all | solution.py:413
  140.7 4.0 %all-to-all-start.8 = ((bf16[16,8,896]{2,1,0:T(8,128)(2,1)}), bf16[16,8,896]{2,1,0:T(8,128)(2,1)S(1)}, u32[]{:S(2)}, u32[]{:S(2)}) async-start(bf16[16,8,896]{2,1,0:T(8,128)(2,1)} %bitcast.15), calls=%async_computation.8 | async-start | bytes 458752 | tf_op jit(solution)/shard_map/all_to_all | solution.py:415
  144.9 12.5 %all-to-all-done.8 = bf16[16,8,896]{2,1,0:T(8,128)(2,1)S(1)} async-done(((bf16[16,8,896]{2,1,0:T(8,128)(2,1)}), bf16[16,8,896]{2,1,0:T(8,128)(2,1)S(1)}, u32[]{:S(2)}, u32[]{:S(2)}) %all-to-all-start.8) | async-done | bytes 229408 | tf_op jit(solution)/shard_map/all_to_all | solution.py:415
  158.1 9.7 %all-to-all-start.9 = ((bf16[8,8,896]{2,1,0:T(8,128)(2,1)}), bf16[8,8,896]{2,1,0:T(8,128)(2,1)S(1)}, u32[]{:S(2)}, u32[]{:S(2)}) async-start(bf16[8,8,896]{2,1,0:T(8,128)(2,1)} %broadcast_in_dim.23), calls=%async_computation.9 | async-start | bytes 229376 | tf_op jit(solution)/shard_map/all_to_all | solution.py:418
  168.4 9.6 %all-to-all-done.9 = bf16[8,8,896]{2,1,0:T(8,128)(2,1)S(1)} async-done(((bf16[8,8,896]{2,1,0:T(8,128)(2,1)}), bf16[8,8,896]{2,1,0:T(8,128)(2,1)S(1)}, u32[]{:S(2)}, u32[]{:S(2)}) %all-to-all-start.9) | async-done | bytes 114720 | tf_op jit(solution)/shard_map/all_to_all | solution.py:418
  177.9 4.1 %all_gather.27 = bf16[64,1792]{1,0:T(8,128)(2,1)S(1)} all-gather(bf16[64,896]{1,0:T(8,128)(2,1)S(1)} %bitcast.37), channel_id=1, replica_groups=mesh['x'=4,'zl'=8,'c'=2,'zh'=2,'y'=4] {'c'}, dimensions={1}, use_global_device_ids=true | all-gather | bytes 344064 | tf_op jit(solution)/shard_map/all_gather | solution.py:419
  (44 shorter events, 23.0 us)
Async XLA Ops:
  0.6 1.0 copy-start
  0.6 19.3 %copy-start.6 = (s32[4]{0:T(128)S(1)}, s32[4]{0:T(128)}, u32[]{:S(2)}) copy-start(s32[4]{0:T(128)} %param.12) | copy-start | bytes 52
  2.5 20.2 %all-to-all-start.4 = ((bf16[4,64,1024]{2,1,0:T(8,128)(2,1)}), bf16[4,64,1024]{2,1,0:T(8,128)(2,1)S(1)}, u32[]{:S(2)}, u32[]{:S(2)}) async-start(bf16[4,64,1024]{2,1,0:T(8,128)(2,1)} %broadcast_in_dim.22), calls=%async_computation.4 | async-start | bytes 1048576 | tf_op jit(solution)/shard_map/all_to_all | solution.py:323
  7.5 23.6 %collective-permute-start.8 = (bf16[64,1024]{1,0:T(8,128)(2,1)S(1)}, bf16[64,1024]{1,0:T(8,128)(2,1)S(1)}, u32[]{:S(2)}, u32[]{:S(2)}) collective-permute-start(bf16[64,1024]{1,0:T(8,128)(2,1)S(1)} %fusion.1), channel_id=1, source_target_pairs={{0,68},{16,84},{32,100},{48,116},{64,4},{80,20},{96,36},{112,52},{... | collective-permute-start | bytes 393224 | tf_op jit(solution)/shard_map/ppermute | solution.py:387
  31.9 12.1 %all-to-all-start.2 = ((bf16[4,64,1024]{2,1,0:T(8,128)(2,1)}), bf16[4,64,1024]{2,1,0:T(8,128)(2,1)S(1)}, u32[]{:S(2)}, u32[]{:S(2)}) async-start(bf16[4,64,1024]{2,1,0:T(8,128)(2,1)} %broadcast_in_dim.7), calls=%async_computation.2 | async-start | bytes 1048576 | tf_op jit(solution)/shard_map/cond/branch_2_fun/all_to_all | solution.py:323
  36.2 27.2 %collective-permute-start.4 = (bf16[272,1024]{1,0:T(8,128)(2,1)S(1)}, bf16[272,1024]{1,0:T(8,128)(2,1)}, u32[]{:S(2)}, u32[]{:S(2)}) collective-permute-start(bf16[272,1024]{1,0:T(8,128)(2,1)S(1)} %get-tuple-element.109), channel_id=1, source_target_pairs={{128,0},{384,128},{0,256},{256,384},{129,1},{385,129},{1,257},{257... | collective-permute-start | bytes 1671176 | tf_op jit(solution)/shard_map/cond/branch_2_fun/ppermute | solution.py:343
  54.3 16.3 %collective-permute-start.5 = (bf16[272,1024]{1,0:T(8,128)(2,1)S(1)}, bf16[272,1024]{1,0:T(8,128)(2,1)}, u32[]{:S(2)}, u32[]{:S(2)}) collective-permute-start(bf16[272,1024]{1,0:T(8,128)(2,1)S(1)} %get-tuple-element.114), channel_id=1, source_target_pairs={{128,0},{384,128},{0,256},{256,384},{129,1},{385,129},{1,257},{257... | collective-permute-start | bytes 1671176 | tf_op jit(solution)/shard_map/cond/branch_2_fun/ppermute | solution.py:348
  58.9 7.0 %copy-start.4 = (bf16[256,128]{1,0:T(8,128)(2,1)}, bf16[256,128]{1,0:T(8,128)(2,1)S(1)}, u32[]{:S(2)}) copy-start(bf16[256,128]{1,0:T(8,128)(2,1)S(1)} %slice.45.ids_ref) | copy-start | bytes 196612 | tf_op jit(solution)/shard_map/cond
  83.0 21.3 %all-to-all-start.6 = ((f32[16,8,256]{2,1,0:T(8,128)}), f32[16,8,256]{2,1,0:T(8,128)S(1)}, u32[]{:S(2)}, u32[]{:S(2)}) async-start(f32[16,8,256]{2,1,0:T(8,128)} %merge_near.1), calls=%async_computation.6 | async-start | bytes 262144 | tf_op jit(solution)/shard_map/all_to_all | solution.py:402
  116.1 5.7 %copy-start.1 = (bf16[1,1792,1024]{2,1,0:T(8,128)(2,1)S(1)}, bf16[1,1792,1024]{2,1,0:T(8,128)(2,1)}, u32[]{:S(2)}) copy-start(bf16[1,1792,1024]{2,1,0:T(8,128)(2,1)} %w_ref.5) | copy-start | bytes 11010052
  119.6 4.4 %collective-permute-start.9 = (bf16[512,896]{1,0:T(8,128)(2,1)S(1)}, bf16[512,896]{1,0:T(8,128)(2,1)S(1)}, u32[]{:S(2)}, u32[]{:S(2)}) collective-permute-start(bf16[512,896]{1,0:T(8,128)(2,1)S(1)} %head_grads.3), channel_id=1, source_target_pairs={{0,8},{8,0},{1,9},{9,1},{2,10},{10,2},{3,11},{11,3},{4,12},{12,4},... | collective-permute-start | bytes 2752520 | tf_op jit(solution)/shard_map/ppermute | solution.py:410
  124.1 20.6 %copy-start.7 = (f32[1,64]{1,0:T(1,128)S(1)}, f32[1,64]{1,0:T(1,128)}, u32[]{:S(2)}) copy-start(f32[1,64]{1,0:T(1,128)} %param.13) | copy-start | bytes 772
  140.7 16.6 %all-to-all-start.8 = ((bf16[16,8,896]{2,1,0:T(8,128)(2,1)}), bf16[16,8,896]{2,1,0:T(8,128)(2,1)S(1)}, u32[]{:S(2)}, u32[]{:S(2)}) async-start(bf16[16,8,896]{2,1,0:T(8,128)(2,1)} %bitcast.15), calls=%async_computation.8 | async-start | bytes 458752 | tf_op jit(solution)/shard_map/all_to_all | solution.py:415
  158.1 19.8 %all-to-all-start.9 = ((bf16[8,8,896]{2,1,0:T(8,128)(2,1)}), bf16[8,8,896]{2,1,0:T(8,128)(2,1)S(1)}, u32[]{:S(2)}, u32[]{:S(2)}) async-start(bf16[8,8,896]{2,1,0:T(8,128)(2,1)} %broadcast_in_dim.23), calls=%async_computation.9 | async-start | bytes 229376 | tf_op jit(solution)/shard_map/all_to_all | solution.py:418

commit v3 on v2

--- a/solution.py
+++ b/solution.py
@@ -21,14 +21,16 @@
 TILE = 32
 
 
-def call(kernel, outs, operands, name, scratch=(), flops=0):
-    scalars = [o.ndim == 1 for o in operands]
+def call(kernel, outs, operands, name, scratch=(), flops=0, stays=()):
     vmem, smem = pl.BlockSpec(memory_space=pltpu.VMEM), pl.BlockSpec(memory_space=pltpu.SMEM)
+    specs = [smem if o.ndim == 1 else vmem for o in operands]
+    for i in stays:
+        specs[i] = pl.BlockSpec(memory_space=pl.ANY)
     moved = sum(o.size * o.dtype.itemsize for o in list(operands) + list(outs))
     return pl.pallas_call(
         kernel,
         out_shape=outs if len(outs) > 1 else outs[0],
-        in_specs=[smem if s else vmem for s in scalars],
+        in_specs=specs,
         out_specs=[vmem] * len(outs) if len(outs) > 1 else vmem,
         scratch_shapes=scratch,
         compiler_params=pltpu.CompilerParams(vmem_limit_bytes=moved + (6 << 20)),
@@ -47,7 +49,7 @@
             body(pl.ds(pl.multiple_of(i * step, step), step))
             return carry
 
-        lax.fori_loop(0, rows // step, at, 0)
+        lax.fori_loop(0, rows // step, at, 0, unroll=True)
 
     return run
 
@@ -61,14 +63,38 @@
     return out
 
 
-def forward_kernel(h_ref, w_ref, x_ref, sent_ref, top_ref):
-    width = w_ref.shape[2]
-    at = pl.ds(pl.multiple_of(pl.program_id(0) * width, width), width)
-    x_ref[:, at] = jnp.dot(h_ref[...], w_ref[0], preferred_element_type=F32)
-
-    @pl.when(pl.program_id(0) == pl.num_programs(0) - 1)
-    def _():
-        below_top(x_ref, sent_ref, top_ref)
+def hold_kernel(w_ref, out_ref, sem):
+    copy = pltpu.make_async_copy(w_ref.at[0, : out_ref.shape[0]], out_ref, sem)
+    copy.start()
+    copy.wait()
+
+
+def hold(head):
+    return pl.pallas_call(
+        hold_kernel,
+        out_shape=jax.ShapeDtypeStruct((head.shape[1] // 2, head.shape[2]), head.dtype),
+        in_specs=[pl.BlockSpec(memory_space=pl.ANY)],
+        out_specs=pl.BlockSpec(memory_space=pltpu.VMEM),
+        scratch_shapes=[pltpu.SemaphoreType.DMA(())],
+        compiler_params=pltpu.CompilerParams(vmem_limit_bytes=8 << 20),
+        cost_estimate=pl.CostEstimate(flops=0, bytes_accessed=4 << 20, transcendentals=0),
+        name="hold_head",
+    )(head)
+
+
+def forward_kernel(h_ref, held_ref, w_ref, x_ref, sent_ref, top_ref, rest_ref, sem):
+    depth = held_ref.shape[0]
+    copy = pltpu.make_async_copy(w_ref.at[0, depth:], rest_ref, sem)
+    copy.start()
+    width = 512
+    for n in range(0, x_ref.shape[1], width):
+        at = slice(n, n + width)
+        x_ref[:, at] = jnp.dot(h_ref[:, :depth], held_ref[:, at], preferred_element_type=F32)
+    copy.wait()
+    for n in range(0, x_ref.shape[1], width):
+        at = slice(n, n + width)
+        x_ref[:, at] += jnp.dot(h_ref[:, depth:], rest_ref[:, at], preferred_element_type=F32)
+    below_top(x_ref, sent_ref, top_ref)
 
 
 def below_top(x_ref, sent_ref, top_ref):
@@ -96,29 +122,25 @@
         sent_ref[rows:, b * LANES : (b + 1) * LANES] = pieces.astype(BF16)
 
 
-def forward(h, head):
-    rows, features, vocab = h.shape[0], h.shape[1], head.shape[2]
-    width = 256
-    outs = [shape(rows, vocab), shape(rows + 16, vocab, dtype=BF16), shape(rows, LANES)]
-    return pl.pallas_call(
+def features_of(block):
+    return lax.all_gather(block[:, : block.shape[1] - LANES], "c", axis=1, tiled=True)
+
+
+def forward(h, held, head):
+    rows, vocab = h.shape[0], head.shape[2]
+    return call(
         forward_kernel,
-        out_shape=outs,
-        grid=(vocab // width,),
-        in_specs=[
-            pl.BlockSpec(h.shape, lambda n: (0, 0)),
-            pl.BlockSpec((1, features, width), lambda n: (0, 0, n)),
-        ],
-        out_specs=[pl.BlockSpec(o.shape, lambda n: (0, 0)) for o in outs],
-        compiler_params=pltpu.CompilerParams(vmem_limit_bytes=16 << 20),
-        cost_estimate=pl.CostEstimate(
-            flops=2 * rows * features * vocab, bytes_accessed=6 << 20, transcendentals=0
-        ),
-        name="logits",
-    )(h, head)
+        [shape(rows, vocab), shape(rows + 16, vocab, dtype=BF16), shape(rows, LANES)],
+        (h, held, head),
+        "logits",
+        [pltpu.VMEM(held.shape, held.dtype), pltpu.SemaphoreType.DMA(())],
+        flops=2 * rows * h.shape[1] * vocab,
+        stays=(2,),
+    )
 
 
 def target_column(ids_ref, at, offset):
-    ids = ids_ref[at].astype(jnp.int32)
+    ids = ids_ref[at, ids_ref.shape[1] - LANES :].astype(jnp.int32)
     lane = lax.broadcasted_iota(jnp.int32, ids.shape, 1)
     ids = jnp.where(lane == 0, ids * 4096, jnp.where(lane == 1, ids * 64, ids))
     return jnp.sum(ids.astype(F32), axis=1, keepdims=True).astype(jnp.int32) - offset
@@ -209,92 +231,50 @@
 
 
 def grad_kernel(
-    where_ref, whole_ref, local_ref, ids_ref, x_near, x_far, got_near, got_far,
+    where_ref, whole_ref, local_ref, near_ids, far_ids, x_near, x_far, got_near, got_far,
     out_ref, loss_ref, flat_ref, cols_ref,
 ):
-    step_at = pl.program_id(0)
-    rows, vocab = out_ref.shape
-    half = whole_ref.shape[2]
-
-    @pl.when(step_at == 0)
-    def _():
-        flat_ref[...] = jnp.zeros_like(flat_ref)
-        loss_ref[...] = jnp.zeros_like(loss_ref)
-        for i in range(2):
-            zh = where_ref[0] if i == 0 else 1 - where_ref[0]
-            lanes = pl.ds(pl.multiple_of(zh * half, half), half)
-            top, total, to_peer, target, peer_top, peer_total, to_own = (
-                whole_ref[zh, k : k + 1, :] for k in range(7)
-            )
-            log_total = top + jnp.log(total)
-            peer_log_total = peer_top + jnp.log(peer_total)
-            step = log_total - peer_log_total
-            reverse = to_peer / total - step
-            forward_kl = to_own / peer_total + step
-            loss_ref[0:1, lanes] = log_total - target + 0.5 * kl_weight * (forward_kl + reverse)
-            own_top, own_peer_top = local_ref[0, 0:1, lanes], local_ref[0, 4:5, lanes]
-            flat_ref[0:1] = jnp.exp(own_top - log_total)
-            flat_ref[1:2] = (0.5 * kl_weight) * jnp.exp(own_peer_top - peer_log_total)
-            flat_ref[2:3] = (1.0 + 0.5 * kl_weight) + 0.5 * kl_weight * (
-                (own_top - own_peer_top) - step - reverse
-            )
-            for b in range(half // LANES):
-                to = i * half + b * LANES
-                cols_ref[to : to + LANES] = jnp.transpose(flat_ref[:, b * LANES : (b + 1) * LANES])
-
-    def block(x_ref, got_ref):
-        column = lax.broadcasted_iota(jnp.int32, (16, vocab), 1)
-
-        @tiles(rows, 16)
-        def _(at):
-            here = pl.ds(pl.multiple_of(step_at * rows + at.start, 16), 16)
+    half, vocab = x_near.shape
+    quarter = half // 4
+    flat_ref[...] = jnp.zeros_like(flat_ref)
+    loss_ref[...] = jnp.zeros_like(loss_ref)
+    column = lax.broadcasted_iota(jnp.int32, (TILE, vocab), 1)
+    halves = (
+        (where_ref[0], near_ids, x_near, got_near),
+        (1 - where_ref[0], far_ids, x_far, got_far),
+    )
+    for zh, ids_ref, x_ref, got_ref in halves:
+        lanes = pl.ds(pl.multiple_of(zh * half, half), half)
+        top, total, to_peer, target, peer_top, peer_total, to_own = (
+            whole_ref[zh, k : k + 1, :] for k in range(7)
+        )
+        log_total = top + jnp.log(total)
+        peer_log_total = peer_top + jnp.log(peer_total)
+        step = log_total - peer_log_total
+        reverse = to_peer / total - step
+        forward_kl = to_own / peer_total + step
+        loss_ref[0:1, lanes] = log_total - target + 0.5 * kl_weight * (forward_kl + reverse)
+        own_top, own_peer_top = local_ref[0, 0:1, lanes], local_ref[0, 4:5, lanes]
+        flat_ref[0:1] = jnp.exp(own_top - log_total)
+        flat_ref[1:2] = (0.5 * kl_weight) * jnp.exp(own_peer_top - peer_log_total)
+        flat_ref[2:3] = (1.0 + 0.5 * kl_weight) + 0.5 * kl_weight * (
+            (own_top - own_peer_top) - step - reverse
+        )
+        for b in range(half // LANES):
+            block = slice(b * LANES, (b + 1) * LANES)
+            cols_ref[block] = jnp.transpose(flat_ref[:, block])
+        for i in range(half // TILE):
+            at = slice(i * TILE, (i + 1) * TILE)
+            y, t = divmod(i * TILE, quarter)
             below = x_ref[at]
             peer_below = -jnp.sqrt(jnp.sqrt(got_ref[at].astype(F32)))
             hit = column == target_column(ids_ref, at, where_ref[1])
-            own_prob = jnp.exp(below) * cols_ref[here, 0:1]
+            own_prob = jnp.exp(below) * cols_ref[at, 0:1]
             gap = below - peer_below
-            inner = own_prob * (cols_ref[here, 2:3] + (0.5 * kl_weight) * gap)
-            inner = inner - jnp.exp(peer_below) * cols_ref[here, 1:2] - jnp.where(hit, 1.0, 0.0)
-            out_ref[at] = inner.astype(BF16)
-
-    pl.when(step_at < 4)(lambda: block(x_near, got_near))
-    pl.when(step_at >= 4)(lambda: block(x_far, got_far))
-
-
-def logit_grads(where, whole, local, ids, x_near, x_far, got_near, got_far):
-    half, vocab = x_near.shape
-    rows = half // 4
-    near = pl.BlockSpec((rows, vocab), lambda n, w: (jnp.minimum(n, 3), 0))
-    far = pl.BlockSpec((rows, vocab), lambda n, w: (jnp.maximum(n - 4, 0), 0))
-
-    def place(n, w):
-        return (2 * (n % 4) + jnp.where(n < 4, w[0], 1 - w[0]), 0)
-
-    return pl.pallas_call(
-        grad_kernel,
-        out_shape=[shape(2 * half, vocab, dtype=BF16), shape(8, 2 * half)],
-        grid_spec=pltpu.PrefetchScalarGridSpec(
-            num_scalar_prefetch=1,
-            grid=(8,),
-            in_specs=[
-                pl.BlockSpec(whole.shape, lambda n, w: (0, 0, 0)),
-                pl.BlockSpec(local.shape, lambda n, w: (0, 0, 0)),
-                pl.BlockSpec((rows, LANES), lambda n, w: (n, 0)),
-                near,
-                far,
-                near,
-                far,
-            ],
-            out_specs=[
-                pl.BlockSpec((rows, vocab), place),
-                pl.BlockSpec((8, 2 * half), lambda n, w: (0, 0)),
-            ],
-            scratch_shapes=[pltpu.VMEM((LANES, half), F32), pltpu.VMEM((2 * half, LANES), F32)],
-        ),
-        compiler_params=pltpu.CompilerParams(vmem_limit_bytes=16 << 20),
-        cost_estimate=pl.CostEstimate(flops=1, bytes_accessed=4 << 20, transcendentals=0),
-        name="logit_grads",
-    )(where, whole, local, ids, x_near, x_far, got_near, got_far)
+            inner = own_prob * (cols_ref[at, 2:3] + (0.5 * kl_weight) * gap)
+            inner = inner - jnp.exp(peer_below) * cols_ref[at, 1:2] - jnp.where(hit, 1.0, 0.0)
+            to = pl.multiple_of(2 * quarter * y + t + zh * quarter, TILE)
+            out_ref[pl.ds(to, TILE)] = inner.astype(BF16)
 
 
 def backward_kernel(half_ref, g_ref, w_ref, out_ref):
@@ -319,16 +299,27 @@
     )
 
 
+def sum_kernel(in_ref, out_ref):
+    total = in_ref[0].astype(F32)
+    for k in range(1, in_ref.shape[0]):
+        total = total + in_ref[k].astype(F32)
+    out_ref[...] = total.astype(BF16)
+
+
+def last_sum_kernel(in_ref, weight_ref, out_ref):
+    total = in_ref[0].astype(F32)
+    for k in range(1, in_ref.shape[0]):
+        total = total + in_ref[k].astype(F32)
+    total = (total * weight_ref[:, 0:1]).astype(BF16)
+    for k in range(out_ref.shape[0]):
+        out_ref[k] = total
+
+
 def spread(block):
     out = lax.all_to_all(jnp.broadcast_to(block[None], (4,) + block.shape), "y", 0, 0)
     return out.reshape(-1, block.shape[1])
 
 
-def logits_of(block, head):
-    h = lax.all_gather(block[:, : head.shape[1] // 2], "c", axis=1, tiled=True)
-    return forward(h, head)
-
-
 def own_of(offset, ids, x, top):
     outs = [shape(*x.shape), shape(x.shape[0], LANES)]
     return call(own_kernel, outs, (offset, ids, x, top), "own_stats")
@@ -336,20 +327,18 @@
 
 def exchange(partner, near, far, head, where):
     to_learner = [(partner[r], r) for r in range(4)]
-    near_ids, x_near, sent, top_near = near
+    near, x_near, sent, top_near = near
     offset = where[1:2]
-    half = x_near.shape[0]
-    depth = head.shape[1] // 2
+    half = near.shape[0]
     got_near = lax.ppermute(sent, "x", to_learner)
-    far_h = spread(far)
-    far_ids = far_h[:, depth:]
-    x_far, sent, top_far = logits_of(far_h, head)
+    far = spread(far)
+    x_far, sent, top_far = forward(features_of(far), hold(head), head)
     sent, x_near = lax.optimization_barrier((sent, x_near))
     got_far = lax.ppermute(sent, "x", to_learner)
-    power_near, cols_near = own_of(offset, near_ids, x_near, top_near)
-    power_far, cols_far = own_of(offset, far_ids, x_far, top_far)
+    power_near, cols_near = own_of(offset, near, x_near, top_near)
+    power_far, cols_far = own_of(offset, far, x_far, top_far)
     scratch = [pltpu.VMEM((half, LANES), F32)]
-    near = call(
+    near_stats = call(
         stats_near_kernel,
         [shape(8, half)],
         (x_near, power_near, cols_near, got_near),
@@ -359,11 +348,11 @@
     local = call(
         stats_far_kernel,
         [shape(8, 8, 2 * half)],
-        (where, near, x_far, power_far, cols_far, got_far),
+        (where, near_stats, x_far, power_far, cols_far, got_far),
         "far_stats",
         scratch,
     )
-    return local, far_ids, x_far, got_near, got_far
+    return local, far, x_near, x_far, got_near, got_far
 
 
 def on_device(hidden, head_weight, targets, pairing, token_weight):
@@ -385,16 +374,15 @@
         axis=1,
     )
     far = lax.ppermute(mine, ("zl", "zh"), SWAP_Z)
-    near_h = spread(mine)
-    near_ids = near_h[:, depth:]
-    x_near, sent, top_near = logits_of(near_h, head_weight)
+    near = spread(mine)
+    x_near, sent, top_near = forward(features_of(near), hold(head_weight), head_weight)
     x_near, far = lax.optimization_barrier((x_near, far))
     first, second = pairing[0], pairing[1]
     which = jnp.where(first == 2, jnp.where(second == 3, 0, 3), jnp.where(first == 3, 1, 2))
-    local, far_ids, x_far, got_near, got_far = lax.switch(
+    local, far, x_near, x_far, got_near, got_far = lax.switch(
         which,
         [functools.partial(exchange, p) for p in PAIRINGS],
-        (near_ids, x_near, sent, top_near), far, head_weight, where,
+        (near, x_near, sent, top_near), far, head_weight, where,
     )
 
     parts = lax.all_to_all(local, ("c", "y"), 0, 0)
@@ -402,8 +390,13 @@
     parts = lax.all_to_all(parts, Z, 0, 0)
     parts = call(last_merge_kernel, [shape(8, half)], (parts,), "merge_all")
     whole = lax.all_gather(parts, "c", axis=0, tiled=False)
-    ids = jnp.concatenate([near_ids, far_ids], axis=0)
-    grads, losses = logit_grads(where, whole, local, ids, x_near, x_far, got_near, got_far)
+    grads, losses = call(
+        grad_kernel,
+        [shape(2 * half, vocab, dtype=BF16), shape(8, 2 * half)],
+        (where, whole, local, near, far, x_near, x_far, got_near, got_far),
+        "logit_grads",
+        [pltpu.VMEM((LANES, half), F32), pltpu.VMEM((half, LANES), F32)],
+    )
     loss = lax.dynamic_slice(losses, (0, zh * half + y * rows), (1, rows))
     loss = token_weight * loss
 
@@ -411,11 +404,16 @@
     kept = backward(core, grads, head_weight, F32)
     by_y = (kept + sent.astype(F32)).astype(BF16).reshape(4, 2 * rows, depth)
     by_y = lax.all_to_all(by_y, "y", 0, 0)
-    by_z = jnp.sum(by_y.astype(F32), axis=0).astype(BF16).reshape(16, rows // 8, depth)
-    by_z = lax.all_to_all(by_z, Z, 0, 0)
+    by_z = call(sum_kernel, [shape(2 * rows, depth, dtype=BF16)], (by_y,), "sum_y")
+    by_z = lax.all_to_all(by_z.reshape(16, rows // 8, depth), Z, 0, 0)
     weights = lax.dynamic_slice_in_dim(token_weight[0], zl * (rows // 8), rows // 8, 0)
-    final = (jnp.sum(by_z.astype(F32), axis=0) * weights[:, None]).astype(BF16)
-    final = lax.all_to_all(jnp.broadcast_to(final[None], (8,) + final.shape), "zl", 0, 0)
+    final = call(
+        last_sum_kernel,
+        [shape(8, rows // 8, depth, dtype=BF16)],
+        (by_z, jnp.broadcast_to(weights[:, None], (rows // 8, LANES))),
+        "sum_z",
+    )
+    final = lax.all_to_all(final, "zl", 0, 0)
     final = lax.all_gather(final.reshape(rows, depth), "c", axis=1, tiled=True)
     return (final[None], loss)
 

time: 184 us -> 178 us (0.967)
  Pallas kernels: 32.6 us -> 26.4 us
  waiting for transfers between devices: 42.4 us -> 44.3 us
    pallas_call x3 -> x2, Pallas kernels: 17.1 us -> 3.02 us  [hold(): pl.pallas_call(hold_kernel, out_shape=jax.ShapeDtypeStruct((head.shape[1]...]
    pallas_call x8 -> x13, Pallas kernels: 15.5 us -> 23.4 us  [call(): pl.pallas_call(kernel, out_shape=outs if len(outs) > 1 else outs[0], in_s...]
    ppermute x1, waiting for transfers between devices: 4.56 us -> 6.45 us  [exchange(): got_far = lax.ppermute(sent, 'x', to_learner)]
  transfers between devices with their start and end apart: 9 -> 9, of which waited for: 7 -> 6; matrix products, arithmetic and copies ran while one was open for 1% -> 1% of each run, Pallas kernels for 10% -> 9%
where the time goes in v3:
time: 178 us; the launch traced here: 177 us
  starting transfers between devices  55.9 us (31%)
  waiting for transfers between devices  44.3 us (25%)
  blocking collectives  40.3 us (23%)
  Pallas kernels  26.4 us (15%)
  local copies, waits for them, and re-layouts  5.24 us (3%)
  between operations  2.76 us (2%)
    pallas_call x13, Pallas kernels, call(): pl.pallas_call(kernel, out_shape=outs if len(outs) > 1 else outs[0], in_s...  23.4 us
    all_to_all x1, blocking collectives, on_device(): by_y = lax.all_to_all(by_y, 'y', 0, 0)  15.7 us
    all_to_all x1, waiting for transfers between devices, on_device(): by_z = lax.all_to_all(by_z.reshape(16, rows // 8, depth), Z, 0, 0)  12.5 us
    ppermute x1, starting transfers between devices, on_device(): far = lax.ppermute(mine, ('zl', 'zh'), SWAP_Z)  12.4 us
    all_to_all x1, waiting for transfers between devices, on_device(): parts = lax.all_to_all(parts, Z, 0, 0)  12.1 us
    all_to_all x1, starting transfers between devices, on_device(): final = lax.all_to_all(final, 'zl', 0, 0)  9.66 us
    all_to_all x1, waiting for transfers between devices, on_device(): final = lax.all_to_all(final, 'zl', 0, 0)  9.56 us
    all_to_all x2, starting transfers between devices, spread(): lax.all_to_all(jnp.broadcast_to(block[None], (4,) + block.shape), 'y', 0, 0)  9.53 us
  transfers between devices with their start and end apart: 9, of which 6 were waited for; matrix products, arithmetic and copies ran while one was open for 1% of the time, Pallas kernels for 9%

profile of v3, /device:TPU:1, one launch (start us, length us, event | category | flops | bytes accessed | tf_op | source)
XLA Modules:
  0.0 177.0 jit_solution(468969934683594632)
XLA Ops:
  2.5 5.0 %all-to-all-start.4 = ((bf16[4,64,1024]{2,1,0:T(8,128)(2,1)}), bf16[4,64,1024]{2,1,0:T(8,128)(2,1)S(1)}, u32[]{:S(2)}, u32[]{:S(2)}) async-start(bf16[4,64,1024]{2,1,0:T(8,128)(2,1)} %broadcast_in_dim.28), calls=%async_computation.4 | async-start | bytes 1048576 | tf_op jit(solution)/shard_map/all_to_all | solution.py:319
  7.5 12.4 %collective-permute-start.8 = (bf16[64,1024]{1,0:T(8,128)(2,1)S(1)}, bf16[64,1024]{1,0:T(8,128)(2,1)S(1)}, u32[]{:S(2)}, u32[]{:S(2)}) collective-permute-start(bf16[64,1024]{1,0:T(8,128)(2,1)S(1)} %fusion.1), channel_id=1, source_target_pairs={{0,68},{16,84},{32,100},{48,116},{64,4},{80,20},{96,36},{112,52},{... | collective-permute-start | bytes 393224 | tf_op jit(solution)/shard_map/ppermute | solution.py:376
  24.9 3.3 %all_gather.24.h_ref = bf16[256,1792]{1,0:T(8,128)(2,1)S(1)} all-gather(bf16[256,896]{1,0:T(8,128)(2,1)S(1)} %slice.28), channel_id=1, replica_groups=mesh['x'=4,'zl'=8,'c'=2,'zh'=2,'y'=4] {'c'}, dimensions={1}, use_global_device_ids=true | all-gather | bytes 1376256 | tf_op jit(solution)/shard_map/all_gather | solution.py:126
  28.2 3.3 %logits.9 = (f32[256,1024]{1,0:T(8,128)S(1)}, bf16[272,1024]{1,0:T(8,128)(2,1)}, f32[256,128]{1,0:T(8,128)S(1)}) custom-call(bf16[256,1792]{1,0:T(8,128)(2,1)S(1)} %all_gather.24.h_ref, bf16[896,1024]{1,0:T(8,128)(2,1)S(1)} %hold_head.9.held_ref, bf16[1,1792,1024]{2,1,0:T(8,128)(2,1)} %w_ref.7), custom_call_target="tpu_custom_call" | custom-call | flops 939524096 | bytes 8159232 | tf_op jit(solution)/shard_map/logits/pallas_call | solution.py:30
  31.6 41.8 %conditional.1 = (f32[8,8,512]{2,1,0:T(8,128)S(1)}, bf16[256,1024]{1,0:T(8,128)(2,1)}, f32[256,1024]{1,0:T(8,128)S(1)}, f32[256,1024]{1,0:T(8,128)}, bf16[272,10...) conditional(s32[]{:T(128)} %bitcast.7, (bf16[64,1024]{1,0:T(8,128)(2,1)S(1)}, ...), branch_computations={%region_0.1_spmd, %region_1.2_spmd, %region_2.3_spmd, %region_3.4_... | conditional | flops 939524096 | bytes 34914508 | solution.py:382
  32.4 4.5 %all-to-all-start.2 = ((bf16[4,64,1024]{2,1,0:T(8,128)(2,1)}), bf16[4,64,1024]{2,1,0:T(8,128)(2,1)}, u32[]{:S(2)}, u32[]{:S(2)}) async-start(bf16[4,64,1024]{2,1,0:T(8,128)(2,1)} %broadcast_in_dim.5), calls=%async_computation.2 | async-start | bytes 1048576 | tf_op jit(solution)/shard_map/cond/branch_2_fun/all_to_all | solution.py:319
  36.9 4.6 %collective-permute-start.4 = (bf16[272,1024]{1,0:T(8,128)(2,1)}, bf16[272,1024]{1,0:T(8,128)(2,1)}, u32[]{:S(2)}, u32[]{:S(2)}) collective-permute-start(bf16[272,1024]{1,0:T(8,128)(2,1)} %get-tuple-element.109), channel_id=1, source_target_pairs={{128,0},{384,128},{0,256},{256,384},{129,1},{385,129},{1,257},{257... | collective-permute-start | bytes 1671176 | tf_op jit(solution)/shard_map/cond/branch_2_fun/ppermute | solution.py:333
  43.1 2.9 %all-to-all-done.2 = bf16[4,64,1024]{2,1,0:T(8,128)(2,1)} async-done(((bf16[4,64,1024]{2,1,0:T(8,128)(2,1)}), bf16[4,64,1024]{2,1,0:T(8,128)(2,1)}, u32[]{:S(2)}, u32[]{:S(2)}) %all-to-all-start.2) | async-done | bytes 524320 | tf_op jit(solution)/shard_map/cond/branch_2_fun/all_to_all | solution.py:319
  47.0 3.6 %all_gather.18.h_ref = bf16[256,1792]{1,0:T(8,128)(2,1)S(1)} all-gather(bf16[256,896]{1,0:T(8,128)(2,1)S(1)} %slice.26), channel_id=1, replica_groups=mesh['x'=4,'zl'=8,'c'=2,'zh'=2,'y'=4] {'c'}, dimensions={1}, use_global_device_ids=true | all-gather | bytes 1376256 | tf_op jit(solution)/shard_map/cond/branch_2_fun/all_gather | solution.py:126
  50.6 3.5 %logits.7 = (f32[256,1024]{1,0:T(8,128)}, bf16[272,1024]{1,0:T(8,128)(2,1)S(1)}, f32[256,128]{1,0:T(8,128)S(1)}) custom-call(bf16[256,1792]{1,0:T(8,128)(2,1)S(1)} %all_gather.18.h_ref, bf16[896,1024]{1,0:T(8,128)(2,1)S(1)} %hold_head.7.held_ref, bf16[1,1792,1024]{2,1,0:T(8,128)(2,1)} %get-tuple-element.100.w_ref), custom_call_target="tpu_custom_call" | custom-call | flops 939524096 | bytes 8159232 | tf_op jit(solution)/shard_map/cond/branch_2_fun/logits/pallas_call | solution.py:30
  54.1 5.0 %collective-permute-start.5 = (bf16[272,1024]{1,0:T(8,128)(2,1)S(1)}, bf16[272,1024]{1,0:T(8,128)(2,1)}, u32[]{:S(2)}, u32[]{:S(2)}) collective-permute-start(bf16[272,1024]{1,0:T(8,128)(2,1)S(1)} %get-tuple-element.114), channel_id=1, source_target_pairs={{128,0},{384,128},{0,256},{256,384},{129,1},{385,129},{1,257},{257... | collective-permute-start | bytes 1671176 | tf_op jit(solution)/shard_map/cond/branch_2_fun/ppermute | solution.py:337
  64.1 6.4 %collective-permute-done.5.got_ref = bf16[272,1024]{1,0:T(8,128)(2,1)} collective-permute-done((bf16[272,1024]{1,0:T(8,128)(2,1)S(1)}, bf16[272,1024]{1,0:T(8,128)(2,1)}, u32[]{:S(2)}, u32[]{:S(2)}) %collective-permute-start.5) | collective-permute-done | bytes 557088 | tf_op jit(solution)/shard_map/cond/branch_2_fun/ppermute | solution.py:337
  70.6 2.3 %far_stats.6 = f32[8,8,512]{2,1,0:T(8,128)S(1)} custom-call(s32[2]{0:T(128)S(1)} %get-tuple-element.98.zh_ref, f32[8,256]{1,0:T(8,128)S(1)} %near_stats.6.near_ref, f32[256,1024]{1,0:T(8,128)} %get-tuple-element.180.x_ref, f32[256,1024]{1,0:T(8,128)S(1)} %get-tuple-element.112.power_ref, f32[256,128]{1,0:T(8,128)S(1)} %get-tuple-element.113.cols_ref, ...), custom_call_target="tpu_custom_call" | custom-call | bytes 2924552 | tf_op jit(solution)/shard_map/cond/branch_2_fun/far_stats/pallas_call | solution.py:30
  73.4 8.7 %all_to_all.46.in_ref = f32[8,8,512]{2,1,0:T(8,128)S(1)} all-to-all(f32[8,8,512]{2,1,0:T(8,128)S(1)} %get-tuple-element.152.local_ref), channel_id=1, replica_groups=mesh['x'=4,'zl'=8,'c'=2,'zh'=2,'y'=4] {'c','y'}, dimensions={0} | all-to-all | bytes 262144 | tf_op jit(solution)/shard_map/all_to_all | solution.py:388
  82.8 8.3 %all-to-all-start.6 = ((f32[16,8,256]{2,1,0:T(8,128)}), f32[16,8,256]{2,1,0:T(8,128)S(1)}, u32[]{:S(2)}, u32[]{:S(2)}) async-start(f32[16,8,256]{2,1,0:T(8,128)} %merge_near.1), calls=%async_computation.6 | async-start | bytes 262144 | tf_op jit(solution)/shard_map/all_to_all | solution.py:390
  91.2 12.1 %all-to-all-done.6.in_ref = f32[16,8,256]{2,1,0:T(8,128)S(1)} async-done(((f32[16,8,256]{2,1,0:T(8,128)}), f32[16,8,256]{2,1,0:T(8,128)S(1)}, u32[]{:S(2)}, u32[]{:S(2)}) %all-to-all-start.6) | async-done | bytes 131104 | tf_op jit(solution)/shard_map/all_to_all | solution.py:390
  103.4 4.7 %all-gather = f32[16,256]{1,0:T(8,128)S(1)} all-gather(f32[8,256]{1,0:T(8,128)S(1)} %merge_all.1), channel_id=2, replica_groups=mesh['x'=4,'zl'=8,'c'=2,'zh'=2,'y'=4] {'c'}, dimensions={0}, use_global_device_ids=true | all-gather | bytes 24576 | tf_op jit(solution)/shard_map/all_gather | solution.py:392
  108.1 4.5 %logit_grads.1 = (bf16[512,1024]{1,0:T(8,128)(2,1)S(1)}, f32[8,512]{1,0:T(8,128)S(1)}) custom-call(s32[2]{0:T(128)S(1)} %pad_add_fusion.where_ref, f32[2,8,256]{2,1,0:T(8,128)S(1)} %bitcast.24, f32[8,8,512]{2,1,0:T(8,128)S(1)} %get-tuple-element.152.local_ref, bf16[256,1024]{1,0:T(8,128)(2,1)} %bitcast.30, bf16[256,1024]{1,0:T(8,128)(2,1)} %get-tuple-element.153.far_ids, ...), custom_call_target="tpu_custom_call" | custom-call | bytes 5472264 | tf_op jit(solution)/shard_map/logit_grads/pallas_call | solution.py:30
  118.5 15.7 %all_to_all.47.in_ref = bf16[4,128,896]{2,1,0:T(8,128)(2,1)S(1)} all-to-all(bf16[4,128,896]{2,1,0:T(8,128)(2,1)S(1)} %bitcast.31), channel_id=1, replica_groups=mesh['x'=4,'zl'=8,'c'=2,'zh'=2,'y'=4] {'y'}, dimensions={0} | all-to-all | bytes 1835008 | tf_op jit(solution)/shard_map/all_to_all | solution.py:406
  135.0 4.0 %all-to-all-start.8 = ((bf16[16,8,896]{2,1,0:T(8,128)(2,1)}), bf16[16,8,896]{2,1,0:T(8,128)(2,1)S(1)}, u32[]{:S(2)}, u32[]{:S(2)}) async-start(bf16[16,8,896]{2,1,0:T(8,128)(2,1)} %bitcast.15), calls=%async_computation.8 | async-start | bytes 458752 | tf_op jit(solution)/shard_map/all_to_all | solution.py:408
  139.1 12.5 %all-to-all-done.8.in_ref = bf16[16,8,896]{2,1,0:T(8,128)(2,1)S(1)} async-done(((bf16[16,8,896]{2,1,0:T(8,128)(2,1)}), bf16[16,8,896]{2,1,0:T(8,128)(2,1)S(1)}, u32[]{:S(2)}, u32[]{:S(2)}) %all-to-all-start.8) | async-done | bytes 229408 | tf_op jit(solution)/shard_map/all_to_all | solution.py:408
  152.4 9.7 %all-to-all-start.9 = ((bf16[8,8,896]{2,1,0:T(8,128)(2,1)}), bf16[8,8,896]{2,1,0:T(8,128)(2,1)S(1)}, u32[]{:S(2)}, u32[]{:S(2)}) async-start(bf16[8,8,896]{2,1,0:T(8,128)(2,1)} %sum_z.1), calls=%async_computation.9 | async-start | bytes 229376 | tf_op jit(solution)/shard_map/all_to_all | solution.py:416
  162.7 9.6 %all-to-all-done.9 = bf16[8,8,896]{2,1,0:T(8,128)(2,1)S(1)} async-done(((bf16[8,8,896]{2,1,0:T(8,128)(2,1)}), bf16[8,8,896]{2,1,0:T(8,128)(2,1)S(1)}, u32[]{:S(2)}, u32[]{:S(2)}) %all-to-all-start.9) | async-done | bytes 114720 | tf_op jit(solution)/shard_map/all_to_all | solution.py:416
  172.2 4.1 %all_gather.27 = bf16[64,1792]{1,0:T(8,128)(2,1)S(1)} all-gather(bf16[64,896]{1,0:T(8,128)(2,1)S(1)} %bitcast.33), channel_id=1, replica_groups=mesh['x'=4,'zl'=8,'c'=2,'zh'=2,'y'=4] {'c'}, dimensions={1}, use_global_device_ids=true | all-gather | bytes 344064 | tf_op jit(solution)/shard_map/all_gather | solution.py:417
  (44 shorter events, 22.7 us)
Async XLA Ops:
  0.6 1.0 copy-start
  2.5 21.6 %all-to-all-start.4 = ((bf16[4,64,1024]{2,1,0:T(8,128)(2,1)}), bf16[4,64,1024]{2,1,0:T(8,128)(2,1)S(1)}, u32[]{:S(2)}, u32[]{:S(2)}) async-start(bf16[4,64,1024]{2,1,0:T(8,128)(2,1)} %broadcast_in_dim.28), calls=%async_computation.4 | async-start | bytes 1048576 | tf_op jit(solution)/shard_map/all_to_all | solution.py:319
  7.5 24.1 %collective-permute-start.8 = (bf16[64,1024]{1,0:T(8,128)(2,1)S(1)}, bf16[64,1024]{1,0:T(8,128)(2,1)S(1)}, u32[]{:S(2)}, u32[]{:S(2)}) collective-permute-start(bf16[64,1024]{1,0:T(8,128)(2,1)S(1)} %fusion.1), channel_id=1, source_target_pairs={{0,68},{16,84},{32,100},{48,116},{64,4},{80,20},{96,36},{112,52},{... | collective-permute-start | bytes 393224 | tf_op jit(solution)/shard_map/ppermute | solution.py:376
  19.9 1.5 copy-start.7
  24.1 0.8 copy-start.2
  32.4 13.5 %all-to-all-start.2 = ((bf16[4,64,1024]{2,1,0:T(8,128)(2,1)}), bf16[4,64,1024]{2,1,0:T(8,128)(2,1)}, u32[]{:S(2)}, u32[]{:S(2)}) async-start(bf16[4,64,1024]{2,1,0:T(8,128)(2,1)} %broadcast_in_dim.5), calls=%async_computation.2 | async-start | bytes 1048576 | tf_op jit(solution)/shard_map/cond/branch_2_fun/all_to_all | solution.py:319
  36.9 25.2 %collective-permute-start.4 = (bf16[272,1024]{1,0:T(8,128)(2,1)}, bf16[272,1024]{1,0:T(8,128)(2,1)}, u32[]{:S(2)}, u32[]{:S(2)}) collective-permute-start(bf16[272,1024]{1,0:T(8,128)(2,1)} %get-tuple-element.109), channel_id=1, source_target_pairs={{128,0},{384,128},{0,256},{256,384},{129,1},{385,129},{1,257},{257... | collective-permute-start | bytes 1671176 | tf_op jit(solution)/shard_map/cond/branch_2_fun/ppermute | solution.py:333
  54.1 7.2 %copy-start.5 = (bf16[256,1024]{1,0:T(8,128)(2,1)S(1)}, bf16[256,1024]{1,0:T(8,128)(2,1)}, u32[]{:S(2)}) copy-start(bf16[256,1024]{1,0:T(8,128)(2,1)} %get-tuple-element.105.ids_ref) | copy-start | bytes 1572868 | tf_op jit(solution)/shard_map/cond
  54.1 16.4 %collective-permute-start.5 = (bf16[272,1024]{1,0:T(8,128)(2,1)S(1)}, bf16[272,1024]{1,0:T(8,128)(2,1)}, u32[]{:S(2)}, u32[]{:S(2)}) collective-permute-start(bf16[272,1024]{1,0:T(8,128)(2,1)S(1)} %get-tuple-element.114), channel_id=1, source_target_pairs={{128,0},{384,128},{0,256},{256,384},{129,1},{385,129},{1,257},{257... | collective-permute-start | bytes 1671176 | tf_op jit(solution)/shard_map/cond/branch_2_fun/ppermute | solution.py:337
  82.8 20.5 %all-to-all-start.6 = ((f32[16,8,256]{2,1,0:T(8,128)}), f32[16,8,256]{2,1,0:T(8,128)S(1)}, u32[]{:S(2)}, u32[]{:S(2)}) async-start(f32[16,8,256]{2,1,0:T(8,128)} %merge_near.1), calls=%async_computation.6 | async-start | bytes 262144 | tf_op jit(solution)/shard_map/all_to_all | solution.py:390
  108.1 4.5 %copy-start.1 = (bf16[1,1792,1024]{2,1,0:T(8,128)(2,1)S(1)}, bf16[1,1792,1024]{2,1,0:T(8,128)(2,1)}, u32[]{:S(2)}) copy-start(bf16[1,1792,1024]{2,1,0:T(8,128)(2,1)} %w_ref.7) | copy-start | bytes 11010052
  113.9 4.4 %collective-permute-start.9 = (bf16[512,896]{1,0:T(8,128)(2,1)S(1)}, bf16[512,896]{1,0:T(8,128)(2,1)S(1)}, u32[]{:S(2)}, u32[]{:S(2)}) collective-permute-start(bf16[512,896]{1,0:T(8,128)(2,1)S(1)} %head_grads.3), channel_id=1, source_target_pairs={{0,8},{8,0},{1,9},{9,1},{2,10},{10,2},{3,11},{11,3},{4,12},{12,4},... | collective-permute-start | bytes 2752520 | tf_op jit(solution)/shard_map/ppermute | solution.py:403
  118.4 20.6 %copy-start.8 = (f32[1,64]{1,0:T(1,128)S(1)}, f32[1,64]{1,0:T(1,128)}, u32[]{:S(2)}) copy-start(f32[1,64]{1,0:T(1,128)} %param.13) | copy-start | bytes 772
  135.0 16.6 %all-to-all-start.8 = ((bf16[16,8,896]{2,1,0:T(8,128)(2,1)}), bf16[16,8,896]{2,1,0:T(8,128)(2,1)S(1)}, u32[]{:S(2)}, u32[]{:S(2)}) async-start(bf16[16,8,896]{2,1,0:T(8,128)(2,1)} %bitcast.15), calls=%async_computation.8 | async-start | bytes 458752 | tf_op jit(solution)/shard_map/all_to_all | solution.py:408
  152.4 19.8 %all-to-all-start.9 = ((bf16[8,8,896]{2,1,0:T(8,128)(2,1)}), bf16[8,8,896]{2,1,0:T(8,128)(2,1)S(1)}, u32[]{:S(2)}, u32[]{:S(2)}) async-start(bf16[8,8,896]{2,1,0:T(8,128)(2,1)} %sum_z.1), calls=%async_computation.9 | async-start | bytes 229376 | tf_op jit(solution)/shard_map/all_to_all | solution.py:416

commit v4 on v3

--- a/solution.py
+++ b/solution.py
@@ -162,12 +162,16 @@
         cols_ref[at] = packed((top, total, None, mine), TILE)
 
 
+def decoded(sent):
+    return -lax.rsqrt(lax.rsqrt(jnp.maximum(sent.astype(F32), 1e-37)))
+
+
 def peer_half(x_ref, power_ref, cols_ref, got_ref, all_ref):
     rows = x_ref.shape[0]
 
     @tiles(rows)
     def _(at):
-        below = -jnp.sqrt(jnp.sqrt(got_ref[at].astype(F32)))
+        below = decoded(got_ref[at])
         gap = x_ref[at] - below
         peer = jnp.exp(below)
         to_peer = jnp.sum(power_ref[at] * gap, axis=1, keepdims=True)
@@ -267,7 +271,7 @@
             at = slice(i * TILE, (i + 1) * TILE)
             y, t = divmod(i * TILE, quarter)
             below = x_ref[at]
-            peer_below = -jnp.sqrt(jnp.sqrt(got_ref[at].astype(F32)))
+            peer_below = decoded(got_ref[at])
             hit = column == target_column(ids_ref, at, where_ref[1])
             own_prob = jnp.exp(below) * cols_ref[at, 0:1]
             gap = below - peer_below

time: 178 us -> 178 us (level)
  waiting for transfers between devices: 44.3 us -> 49 us
  starting transfers between devices: 55.9 us -> 52.4 us
    ppermute x1, waiting for transfers between devices: 6.45 us -> 9.62 us  [exchange(): got_far = lax.ppermute(sent, 'x', to_learner)]
where the time goes in v4:
time: 178 us; the launch traced here: 177 us
  starting transfers between devices  52.4 us (29%)
  waiting for transfers between devices  49 us (28%)
  blocking collectives  40.3 us (23%)
  Pallas kernels  25.2 us (14%)
  local copies, waits for them, and re-layouts  5.24 us (3%)
  between operations  2.76 us (2%)
    pallas_call x13, Pallas kernels, call(): pl.pallas_call(kernel, out_shape=outs if len(outs) > 1 else outs[0], in_s...  22.2 us
    all_to_all x1, blocking collectives, on_device(): by_y = lax.all_to_all(by_y, 'y', 0, 0)  15.7 us
    all_to_all x1, waiting for transfers between devices, on_device(): by_z = lax.all_to_all(by_z.reshape(16, rows // 8, depth), Z, 0, 0)  12.5 us
    ppermute x1, starting transfers between devices, on_device(): far = lax.ppermute(mine, ('zl', 'zh'), SWAP_Z)  12.4 us
    all_to_all x1, waiting for transfers between devices, on_device(): parts = lax.all_to_all(parts, Z, 0, 0)  12.1 us
    all_to_all x1, starting transfers between devices, on_device(): final = lax.all_to_all(final, 'zl', 0, 0)  9.66 us
    ppermute x1, waiting for transfers between devices, exchange(): got_far = lax.ppermute(sent, 'x', to_learner)  9.62 us
    all_to_all x1, waiting for transfers between devices, on_device(): final = lax.all_to_all(final, 'zl', 0, 0)  9.56 us
  transfers between devices with their start and end apart: 9, of which 6 were waited for; matrix products, arithmetic and copies ran while one was open for 1% of the time, Pallas kernels for 9%

profile of v4, /device:TPU:1, one launch (start us, length us, event | category | flops | bytes accessed | tf_op | source)
XLA Modules:
  0.0 177.0 jit_solution(4756134248237879392)
XLA Ops:
  2.5 5.0 %all-to-all-start.4 = ((bf16[4,64,1024]{2,1,0:T(8,128)(2,1)}), bf16[4,64,1024]{2,1,0:T(8,128)(2,1)S(1)}, u32[]{:S(2)}, u32[]{:S(2)}) async-start(bf16[4,64,1024]{2,1,0:T(8,128)(2,1)} %broadcast_in_dim.28), calls=%async_computation.4 | async-start | bytes 1048576 | tf_op jit(solution)/shard_map/all_to_all | solution.py:323
  7.5 12.4 %collective-permute-start.8 = (bf16[64,1024]{1,0:T(8,128)(2,1)S(1)}, bf16[64,1024]{1,0:T(8,128)(2,1)S(1)}, u32[]{:S(2)}, u32[]{:S(2)}) collective-permute-start(bf16[64,1024]{1,0:T(8,128)(2,1)S(1)} %fusion.1), channel_id=1, source_target_pairs={{0,68},{16,84},{32,100},{48,116},{64,4},{80,20},{96,36},{112,52},{... | collective-permute-start | bytes 393224 | tf_op jit(solution)/shard_map/ppermute | solution.py:380
  24.9 3.3 %all_gather.24.h_ref = bf16[256,1792]{1,0:T(8,128)(2,1)S(1)} all-gather(bf16[256,896]{1,0:T(8,128)(2,1)S(1)} %slice.28), channel_id=1, replica_groups=mesh['x'=4,'zl'=8,'c'=2,'zh'=2,'y'=4] {'c'}, dimensions={1}, use_global_device_ids=true | all-gather | bytes 1376256 | tf_op jit(solution)/shard_map/all_gather | solution.py:126
  28.2 3.3 %logits.9 = (f32[256,1024]{1,0:T(8,128)S(1)}, bf16[272,1024]{1,0:T(8,128)(2,1)}, f32[256,128]{1,0:T(8,128)S(1)}) custom-call(bf16[256,1792]{1,0:T(8,128)(2,1)S(1)} %all_gather.24.h_ref, bf16[896,1024]{1,0:T(8,128)(2,1)S(1)} %hold_head.9.held_ref, bf16[1,1792,1024]{2,1,0:T(8,128)(2,1)} %w_ref.7), custom_call_target="tpu_custom_call" | custom-call | flops 939524096 | bytes 8159232 | tf_op jit(solution)/shard_map/logits/pallas_call | solution.py:30
  31.6 42.4 %conditional.1 = (f32[8,8,512]{2,1,0:T(8,128)S(1)}, bf16[256,1024]{1,0:T(8,128)(2,1)}, f32[256,1024]{1,0:T(8,128)S(1)}, f32[256,1024]{1,0:T(8,128)}, bf16[272,10...) conditional(s32[]{:T(128)} %bitcast.7, (bf16[64,1024]{1,0:T(8,128)(2,1)S(1)}, ...), branch_computations={%region_0.1_spmd, %region_1.2_spmd, %region_2.3_spmd, %region_3.4_... | conditional | flops 939524096 | bytes 34914508 | solution.py:386
  32.6 4.5 %all-to-all-start.3 = ((bf16[4,64,1024]{2,1,0:T(8,128)(2,1)}), bf16[4,64,1024]{2,1,0:T(8,128)(2,1)}, u32[]{:S(2)}, u32[]{:S(2)}) async-start(bf16[4,64,1024]{2,1,0:T(8,128)(2,1)} %broadcast_in_dim.7), calls=%async_computation.3 | async-start | bytes 1048576 | tf_op jit(solution)/shard_map/cond/branch_3_fun/all_to_all | solution.py:323
  37.1 3.1 %collective-permute-start.6 = (bf16[272,1024]{1,0:T(8,128)(2,1)}, bf16[272,1024]{1,0:T(8,128)(2,1)}, u32[]{:S(2)}, u32[]{:S(2)}) collective-permute-start(bf16[272,1024]{1,0:T(8,128)(2,1)} %get-tuple-element.126), channel_id=1, source_target_pairs={{256,0},{0,128},{384,256},{128,384},{257,1},{1,129},{385,257},{129... | collective-permute-start | bytes 1671176 | tf_op jit(solution)/shard_map/cond/branch_3_fun/ppermute | solution.py:337
  41.8 4.4 %all-to-all-done.3 = bf16[4,64,1024]{2,1,0:T(8,128)(2,1)} async-done(((bf16[4,64,1024]{2,1,0:T(8,128)(2,1)}), bf16[4,64,1024]{2,1,0:T(8,128)(2,1)}, u32[]{:S(2)}, u32[]{:S(2)}) %all-to-all-start.3) | async-done | bytes 524320 | tf_op jit(solution)/shard_map/cond/branch_3_fun/all_to_all | solution.py:323
  47.2 3.6 %all_gather.19.h_ref = bf16[256,1792]{1,0:T(8,128)(2,1)S(1)} all-gather(bf16[256,896]{1,0:T(8,128)(2,1)S(1)} %slice.27), channel_id=1, replica_groups=mesh['x'=4,'zl'=8,'c'=2,'zh'=2,'y'=4] {'c'}, dimensions={1}, use_global_device_ids=true | all-gather | bytes 1376256 | tf_op jit(solution)/shard_map/cond/branch_3_fun/all_gather | solution.py:126
  50.8 3.5 %logits.8 = (f32[256,1024]{1,0:T(8,128)}, bf16[272,1024]{1,0:T(8,128)(2,1)S(1)}, f32[256,128]{1,0:T(8,128)S(1)}) custom-call(bf16[256,1792]{1,0:T(8,128)(2,1)S(1)} %all_gather.19.h_ref, bf16[896,1024]{1,0:T(8,128)(2,1)S(1)} %hold_head.8.held_ref, bf16[1,1792,1024]{2,1,0:T(8,128)(2,1)} %get-tuple-element.117.w_ref), custom_call_target="tpu_custom_call" | custom-call | flops 939524096 | bytes 8159232 | tf_op jit(solution)/shard_map/cond/branch_3_fun/logits/pallas_call | solution.py:30
  54.3 3.2 %collective-permute-start.7 = (bf16[272,1024]{1,0:T(8,128)(2,1)S(1)}, bf16[272,1024]{1,0:T(8,128)(2,1)}, u32[]{:S(2)}, u32[]{:S(2)}) collective-permute-start(bf16[272,1024]{1,0:T(8,128)(2,1)S(1)} %get-tuple-element.131), channel_id=1, source_target_pairs={{256,0},{0,128},{384,256},{128,384},{257,1},{1,129},{385,257},{129... | collective-permute-start | bytes 1671176 | tf_op jit(solution)/shard_map/cond/branch_3_fun/ppermute | solution.py:341
  62.2 9.6 %collective-permute-done.7.got_ref = bf16[272,1024]{1,0:T(8,128)(2,1)} collective-permute-done((bf16[272,1024]{1,0:T(8,128)(2,1)S(1)}, bf16[272,1024]{1,0:T(8,128)(2,1)}, u32[]{:S(2)}, u32[]{:S(2)}) %collective-permute-start.7) | collective-permute-done | bytes 557088 | tf_op jit(solution)/shard_map/cond/branch_3_fun/ppermute | solution.py:341
  74.0 8.7 %all_to_all.46.in_ref = f32[8,8,512]{2,1,0:T(8,128)S(1)} all-to-all(f32[8,8,512]{2,1,0:T(8,128)S(1)} %get-tuple-element.152.local_ref), channel_id=1, replica_groups=mesh['x'=4,'zl'=8,'c'=2,'zh'=2,'y'=4] {'c','y'}, dimensions={0} | all-to-all | bytes 262144 | tf_op jit(solution)/shard_map/all_to_all | solution.py:392
  83.5 8.2 %all-to-all-start.6 = ((f32[16,8,256]{2,1,0:T(8,128)}), f32[16,8,256]{2,1,0:T(8,128)S(1)}, u32[]{:S(2)}, u32[]{:S(2)}) async-start(f32[16,8,256]{2,1,0:T(8,128)} %merge_near.1), calls=%async_computation.6 | async-start | bytes 262144 | tf_op jit(solution)/shard_map/all_to_all | solution.py:394
  91.6 12.1 %all-to-all-done.6.in_ref = f32[16,8,256]{2,1,0:T(8,128)S(1)} async-done(((f32[16,8,256]{2,1,0:T(8,128)}), f32[16,8,256]{2,1,0:T(8,128)S(1)}, u32[]{:S(2)}, u32[]{:S(2)}) %all-to-all-start.6) | async-done | bytes 131104 | tf_op jit(solution)/shard_map/all_to_all | solution.py:394
  103.9 4.7 %all-gather = f32[16,256]{1,0:T(8,128)S(1)} all-gather(f32[8,256]{1,0:T(8,128)S(1)} %merge_all.1), channel_id=2, replica_groups=mesh['x'=4,'zl'=8,'c'=2,'zh'=2,'y'=4] {'c'}, dimensions={0}, use_global_device_ids=true | all-gather | bytes 24576 | tf_op jit(solution)/shard_map/all_gather | solution.py:396
  108.6 3.9 %logit_grads.1 = (bf16[512,1024]{1,0:T(8,128)(2,1)S(1)}, f32[8,512]{1,0:T(8,128)S(1)}) custom-call(s32[2]{0:T(128)S(1)} %pad_add_fusion.where_ref, f32[2,8,256]{2,1,0:T(8,128)S(1)} %bitcast.24, f32[8,8,512]{2,1,0:T(8,128)S(1)} %get-tuple-element.152.local_ref, bf16[256,1024]{1,0:T(8,128)(2,1)} %bitcast.30, bf16[256,1024]{1,0:T(8,128)(2,1)} %get-tuple-element.153.far_ids, ...), custom_call_target="tpu_custom_call" | custom-call | bytes 5472264 | tf_op jit(solution)/shard_map/logit_grads/pallas_call | solution.py:30
  113.8 2.2 %collective-permute-start.9 = (bf16[512,896]{1,0:T(8,128)(2,1)S(1)}, bf16[512,896]{1,0:T(8,128)(2,1)S(1)}, u32[]{:S(2)}, u32[]{:S(2)}) collective-permute-start(bf16[512,896]{1,0:T(8,128)(2,1)S(1)} %head_grads.3), channel_id=1, source_target_pairs={{0,8},{8,0},{1,9},{9,1},{2,10},{10,2},{3,11},{11,3},{4,12},{12,4},... | collective-permute-start | bytes 2752520 | tf_op jit(solution)/shard_map/ppermute | solution.py:407
  118.4 15.7 %all_to_all.47.in_ref = bf16[4,128,896]{2,1,0:T(8,128)(2,1)S(1)} all-to-all(bf16[4,128,896]{2,1,0:T(8,128)(2,1)S(1)} %bitcast.31), channel_id=1, replica_groups=mesh['x'=4,'zl'=8,'c'=2,'zh'=2,'y'=4] {'y'}, dimensions={0} | all-to-all | bytes 1835008 | tf_op jit(solution)/shard_map/all_to_all | solution.py:410
  134.9 4.0 %all-to-all-start.8 = ((bf16[16,8,896]{2,1,0:T(8,128)(2,1)}), bf16[16,8,896]{2,1,0:T(8,128)(2,1)S(1)}, u32[]{:S(2)}, u32[]{:S(2)}) async-start(bf16[16,8,896]{2,1,0:T(8,128)(2,1)} %bitcast.15), calls=%async_computation.8 | async-start | bytes 458752 | tf_op jit(solution)/shard_map/all_to_all | solution.py:412
  139.0 12.5 %all-to-all-done.8.in_ref = bf16[16,8,896]{2,1,0:T(8,128)(2,1)S(1)} async-done(((bf16[16,8,896]{2,1,0:T(8,128)(2,1)}), bf16[16,8,896]{2,1,0:T(8,128)(2,1)S(1)}, u32[]{:S(2)}, u32[]{:S(2)}) %all-to-all-start.8) | async-done | bytes 229408 | tf_op jit(solution)/shard_map/all_to_all | solution.py:412
  152.4 9.7 %all-to-all-start.9 = ((bf16[8,8,896]{2,1,0:T(8,128)(2,1)}), bf16[8,8,896]{2,1,0:T(8,128)(2,1)S(1)}, u32[]{:S(2)}, u32[]{:S(2)}) async-start(bf16[8,8,896]{2,1,0:T(8,128)(2,1)} %sum_z.1), calls=%async_computation.9 | async-start | bytes 229376 | tf_op jit(solution)/shard_map/all_to_all | solution.py:420
  162.6 9.6 %all-to-all-done.9 = bf16[8,8,896]{2,1,0:T(8,128)(2,1)S(1)} async-done(((bf16[8,8,896]{2,1,0:T(8,128)(2,1)}), bf16[8,8,896]{2,1,0:T(8,128)(2,1)S(1)}, u32[]{:S(2)}, u32[]{:S(2)}) %all-to-all-start.9) | async-done | bytes 114720 | tf_op jit(solution)/shard_map/all_to_all | solution.py:420
  172.2 4.1 %all_gather.27 = bf16[64,1792]{1,0:T(8,128)(2,1)S(1)} all-gather(bf16[64,896]{1,0:T(8,128)(2,1)S(1)} %bitcast.33), channel_id=1, replica_groups=mesh['x'=4,'zl'=8,'c'=2,'zh'=2,'y'=4] {'c'}, dimensions={1}, use_global_device_ids=true | all-gather | bytes 344064 | tf_op jit(solution)/shard_map/all_gather | solution.py:421
  (44 shorter events, 22.1 us)
Async XLA Ops:
  0.6 1.0 copy-start
  2.5 21.6 %all-to-all-start.4 = ((bf16[4,64,1024]{2,1,0:T(8,128)(2,1)}), bf16[4,64,1024]{2,1,0:T(8,128)(2,1)S(1)}, u32[]{:S(2)}, u32[]{:S(2)}) async-start(bf16[4,64,1024]{2,1,0:T(8,128)(2,1)} %broadcast_in_dim.28), calls=%async_computation.4 | async-start | bytes 1048576 | tf_op jit(solution)/shard_map/all_to_all | solution.py:323
  7.5 24.1 %collective-permute-start.8 = (bf16[64,1024]{1,0:T(8,128)(2,1)S(1)}, bf16[64,1024]{1,0:T(8,128)(2,1)S(1)}, u32[]{:S(2)}, u32[]{:S(2)}) collective-permute-start(bf16[64,1024]{1,0:T(8,128)(2,1)S(1)} %fusion.1), channel_id=1, source_target_pairs={{0,68},{16,84},{32,100},{48,116},{64,4},{80,20},{96,36},{112,52},{... | collective-permute-start | bytes 393224 | tf_op jit(solution)/shard_map/ppermute | solution.py:380
  19.9 1.5 copy-start.7
  24.1 0.8 copy-start.2
  32.6 13.5 %all-to-all-start.3 = ((bf16[4,64,1024]{2,1,0:T(8,128)(2,1)}), bf16[4,64,1024]{2,1,0:T(8,128)(2,1)}, u32[]{:S(2)}, u32[]{:S(2)}) async-start(bf16[4,64,1024]{2,1,0:T(8,128)(2,1)} %broadcast_in_dim.7), calls=%async_computation.3 | async-start | bytes 1048576 | tf_op jit(solution)/shard_map/cond/branch_3_fun/all_to_all | solution.py:323
  37.1 23.4 %collective-permute-start.6 = (bf16[272,1024]{1,0:T(8,128)(2,1)}, bf16[272,1024]{1,0:T(8,128)(2,1)}, u32[]{:S(2)}, u32[]{:S(2)}) collective-permute-start(bf16[272,1024]{1,0:T(8,128)(2,1)} %get-tuple-element.126), channel_id=1, source_target_pairs={{256,0},{0,128},{384,256},{128,384},{257,1},{1,129},{385,257},{129... | collective-permute-start | bytes 1671176 | tf_op jit(solution)/shard_map/cond/branch_3_fun/ppermute | solution.py:337
  54.3 5.4 %copy-start.6 = (bf16[256,1024]{1,0:T(8,128)(2,1)S(1)}, bf16[256,1024]{1,0:T(8,128)(2,1)}, u32[]{:S(2)}) copy-start(bf16[256,1024]{1,0:T(8,128)(2,1)} %get-tuple-element.122.ids_ref) | copy-start | bytes 1572868 | tf_op jit(solution)/shard_map/cond
  54.3 17.5 %collective-permute-start.7 = (bf16[272,1024]{1,0:T(8,128)(2,1)S(1)}, bf16[272,1024]{1,0:T(8,128)(2,1)}, u32[]{:S(2)}, u32[]{:S(2)}) collective-permute-start(bf16[272,1024]{1,0:T(8,128)(2,1)S(1)} %get-tuple-element.131), channel_id=1, source_target_pairs={{256,0},{0,128},{384,256},{128,384},{257,1},{1,129},{385,257},{129... | collective-permute-start | bytes 1671176 | tf_op jit(solution)/shard_map/cond/branch_3_fun/ppermute | solution.py:341
  83.5 20.3 %all-to-all-start.6 = ((f32[16,8,256]{2,1,0:T(8,128)}), f32[16,8,256]{2,1,0:T(8,128)S(1)}, u32[]{:S(2)}, u32[]{:S(2)}) async-start(f32[16,8,256]{2,1,0:T(8,128)} %merge_near.1), calls=%async_computation.6 | async-start | bytes 262144 | tf_op jit(solution)/shard_map/all_to_all | solution.py:394
  108.6 4.0 %copy-start.1 = (bf16[1,1792,1024]{2,1,0:T(8,128)(2,1)S(1)}, bf16[1,1792,1024]{2,1,0:T(8,128)(2,1)}, u32[]{:S(2)}) copy-start(bf16[1,1792,1024]{2,1,0:T(8,128)(2,1)} %w_ref.7) | copy-start | bytes 11010052
  113.8 4.4 %collective-permute-start.9 = (bf16[512,896]{1,0:T(8,128)(2,1)S(1)}, bf16[512,896]{1,0:T(8,128)(2,1)S(1)}, u32[]{:S(2)}, u32[]{:S(2)}) collective-permute-start(bf16[512,896]{1,0:T(8,128)(2,1)S(1)} %head_grads.3), channel_id=1, source_target_pairs={{0,8},{8,0},{1,9},{9,1},{2,10},{10,2},{3,11},{11,3},{4,12},{12,4},... | collective-permute-start | bytes 2752520 | tf_op jit(solution)/shard_map/ppermute | solution.py:407
  118.4 20.6 %copy-start.8 = (f32[1,64]{1,0:T(1,128)S(1)}, f32[1,64]{1,0:T(1,128)}, u32[]{:S(2)}) copy-start(f32[1,64]{1,0:T(1,128)} %param.13) | copy-start | bytes 772
  134.9 16.6 %all-to-all-start.8 = ((bf16[16,8,896]{2,1,0:T(8,128)(2,1)}), bf16[16,8,896]{2,1,0:T(8,128)(2,1)S(1)}, u32[]{:S(2)}, u32[]{:S(2)}) async-start(bf16[16,8,896]{2,1,0:T(8,128)(2,1)} %bitcast.15), calls=%async_computation.8 | async-start | bytes 458752 | tf_op jit(solution)/shard_map/all_to_all | solution.py:412
  152.4 19.8 %all-to-all-start.9 = ((bf16[8,8,896]{2,1,0:T(8,128)(2,1)}), bf16[8,8,896]{2,1,0:T(8,128)(2,1)S(1)}, u32[]{:S(2)}, u32[]{:S(2)}) async-start(bf16[8,8,896]{2,1,0:T(8,128)(2,1)} %sum_z.1), calls=%async_computation.9 | async-start | bytes 229376 | tf_op jit(solution)/shard_map/all_to_all | solution.py:420

commit v5 on v4

--- a/solution.py
+++ b/solution.py
@@ -82,7 +82,7 @@
     )(head)
 
 
-def forward_kernel(h_ref, held_ref, w_ref, x_ref, sent_ref, top_ref, rest_ref, sem):
+def forward_kernel(h_ref, held_ref, w_ref, x_ref, first_ref, second_ref, top_ref, rest_ref, sem):
     depth = held_ref.shape[0]
     copy = pltpu.make_async_copy(w_ref.at[0, depth:], rest_ref, sem)
     copy.start()
@@ -94,24 +94,32 @@
     for n in range(0, x_ref.shape[1], width):
         at = slice(n, n + width)
         x_ref[:, at] += jnp.dot(h_ref[:, depth:], rest_ref[:, at], preferred_element_type=F32)
-    below_top(x_ref, sent_ref, top_ref)
-
-
-def below_top(x_ref, sent_ref, top_ref):
+    below_top(x_ref, first_ref, second_ref, top_ref)
+
+
+def rows_of(first_ref, second_ref, i):
+    count = first_ref.shape[0] // TILE
+    ref = first_ref if i < count else second_ref
+    return ref, slice(i % count * TILE, (i % count + 1) * TILE)
+
+
+def below_top(x_ref, first_ref, second_ref, top_ref):
     rows, vocab = x_ref.shape
 
-    @tiles(rows)
-    def _(at):
+    for i in range(rows // TILE):
+        at = slice(i * TILE, (i + 1) * TILE)
+        part_ref, part_at = rows_of(first_ref, second_ref, i)
         logits = x_ref[at]
         top = jnp.max(logits, axis=1, keepdims=True)
         below = logits - top
         x_ref[at] = below
         square = below * below
-        sent_ref[at] = (square * square).astype(BF16)
+        part_ref[part_at] = (square * square).astype(BF16)
         top_ref[at] = jnp.broadcast_to(top, (TILE, LANES))
 
     row = lax.broadcasted_iota(jnp.int32, (16, LANES), 0)
-    sent_ref[rows:] = jnp.zeros((16, vocab), BF16)
+    end = rows // 2
+    second_ref[end:] = jnp.zeros((16, vocab), BF16)
     for b in range(rows // LANES):
         top = jnp.transpose(top_ref[b * LANES : (b + 1) * LANES])[:16]
         high = top.astype(BF16).astype(F32)
@@ -119,7 +127,7 @@
         low = (top - high) - middle
         pieces = jnp.where(row == 0, high, jnp.where(row == 1, middle, low))
         pieces = jnp.where(row < 3, pieces, 0.0)
-        sent_ref[rows:, b * LANES : (b + 1) * LANES] = pieces.astype(BF16)
+        second_ref[end:, b * LANES : (b + 1) * LANES] = pieces.astype(BF16)
 
 
 def features_of(block):
@@ -130,7 +138,12 @@
     rows, vocab = h.shape[0], head.shape[2]
     return call(
         forward_kernel,
-        [shape(rows, vocab), shape(rows + 16, vocab, dtype=BF16), shape(rows, LANES)],
+        [
+            shape(rows, vocab),
+            shape(rows // 2, vocab, dtype=BF16),
+            shape(rows // 2 + 16, vocab, dtype=BF16),
+            shape(rows, LANES),
+        ],
         (h, held, head),
         "logits",
         [pltpu.VMEM(held.shape, held.dtype), pltpu.SemaphoreType.DMA(())],
@@ -166,12 +179,14 @@
     return -lax.rsqrt(lax.rsqrt(jnp.maximum(sent.astype(F32), 1e-37)))
 
 
-def peer_half(x_ref, power_ref, cols_ref, got_ref, all_ref):
+def peer_half(x_ref, power_ref, cols_ref, first_ref, second_ref, all_ref):
     rows = x_ref.shape[0]
-
-    @tiles(rows)
-    def _(at):
-        below = decoded(got_ref[at])
+    end = rows // 2
+
+    for i in range(rows // TILE):
+        at = slice(i * TILE, (i + 1) * TILE)
+        part_ref, part_at = rows_of(first_ref, second_ref, i)
+        below = decoded(part_ref[part_at])
         gap = x_ref[at] - below
         peer = jnp.exp(below)
         to_peer = jnp.sum(power_ref[at] * gap, axis=1, keepdims=True)
@@ -184,7 +199,7 @@
         lanes = slice(b * LANES, (b + 1) * LANES)
         flat = jnp.transpose(all_ref[lanes])
         top, total = flat[0:1], flat[1:2]
-        high, middle, low = (got_ref[rows : rows + 16, lanes].astype(F32)[i : i + 1] for i in range(3))
+        high, middle, low = (second_ref[end : end + 16, lanes].astype(F32)[i : i + 1] for i in range(3))
         peer_top = high + (middle + low)
         step = top - peer_top
         row = lax.broadcasted_iota(jnp.int32, (8, LANES), 0)
@@ -195,13 +210,15 @@
     return jnp.concatenate(parts, axis=1)
 
 
-def stats_near_kernel(x_ref, power_ref, cols_ref, got_ref, out_ref, all_ref):
-    out_ref[...] = peer_half(x_ref, power_ref, cols_ref, got_ref, all_ref)
-
-
-def stats_far_kernel(zh_ref, near_ref, x_ref, power_ref, cols_ref, got_ref, out_ref, all_ref):
+def stats_near_kernel(x_ref, power_ref, cols_ref, first_ref, second_ref, out_ref, all_ref):
+    out_ref[...] = peer_half(x_ref, power_ref, cols_ref, first_ref, second_ref, all_ref)
+
+
+def stats_far_kernel(
+    zh_ref, near_ref, x_ref, power_ref, cols_ref, first_ref, second_ref, out_ref, all_ref
+):
     rows = x_ref.shape[0]
-    far = peer_half(x_ref, power_ref, cols_ref, got_ref, all_ref)
+    far = peer_half(x_ref, power_ref, cols_ref, first_ref, second_ref, all_ref)
     near_at = pl.ds(pl.multiple_of(zh_ref[0] * rows, rows), rows)
     far_at = pl.ds(pl.multiple_of((1 - zh_ref[0]) * rows, rows), rows)
     near = near_ref[...]
@@ -235,8 +252,8 @@
 
 
 def grad_kernel(
-    where_ref, whole_ref, local_ref, near_ids, far_ids, x_near, x_far, got_near, got_far,
-    out_ref, loss_ref, flat_ref, cols_ref,
+    where_ref, whole_ref, local_ref, near_ids, far_ids, x_near, x_far,
+    near_first, near_second, far_first, far_second, out_ref, loss_ref, flat_ref, cols_ref,
 ):
     half, vocab = x_near.shape
     quarter = half // 4
@@ -244,10 +261,10 @@
     loss_ref[...] = jnp.zeros_like(loss_ref)
     column = lax.broadcasted_iota(jnp.int32, (TILE, vocab), 1)
     halves = (
-        (where_ref[0], near_ids, x_near, got_near),
-        (1 - where_ref[0], far_ids, x_far, got_far),
-    )
-    for zh, ids_ref, x_ref, got_ref in halves:
+        (where_ref[0], near_ids, x_near, (near_first, near_second)),
+        (1 - where_ref[0], far_ids, x_far, (far_first, far_second)),
+    )
+    for zh, ids_ref, x_ref, got_refs in halves:
         lanes = pl.ds(pl.multiple_of(zh * half, half), half)
         top, total, to_peer, target, peer_top, peer_total, to_own = (
             whole_ref[zh, k : k + 1, :] for k in range(7)
@@ -271,7 +288,8 @@
             at = slice(i * TILE, (i + 1) * TILE)
             y, t = divmod(i * TILE, quarter)
             below = x_ref[at]
-            peer_below = decoded(got_ref[at])
+            part_ref, part_at = rows_of(*got_refs, i)
+            peer_below = decoded(part_ref[part_at])
             hit = column == target_column(ids_ref, at, where_ref[1])
             own_prob = jnp.exp(below) * cols_ref[at, 0:1]
             gap = below - peer_below
@@ -334,25 +352,25 @@
     near, x_near, sent, top_near = near
     offset = where[1:2]
     half = near.shape[0]
-    got_near = lax.ppermute(sent, "x", to_learner)
+    got_near = [lax.ppermute(p, "x", to_learner) for p in sent]
     far = spread(far)
-    x_far, sent, top_far = forward(features_of(far), hold(head), head)
+    x_far, *sent, top_far = forward(features_of(far), hold(head), head)
     sent, x_near = lax.optimization_barrier((sent, x_near))
-    got_far = lax.ppermute(sent, "x", to_learner)
+    got_far = [lax.ppermute(p, "x", to_learner) for p in sent]
     power_near, cols_near = own_of(offset, near, x_near, top_near)
     power_far, cols_far = own_of(offset, far, x_far, top_far)
     scratch = [pltpu.VMEM((half, LANES), F32)]
     near_stats = call(
         stats_near_kernel,
         [shape(8, half)],
-        (x_near, power_near, cols_near, got_near),
+        (x_near, power_near, cols_near, *got_near),
         "near_stats",
         scratch,
     )
     local = call(
         stats_far_kernel,
         [shape(8, 8, 2 * half)],
-        (where, near_stats, x_far, power_far, cols_far, got_far),
+        (where, near_stats, x_far, power_far, cols_far, *got_far),
         "far_stats",
         scratch,
     )
@@ -379,7 +397,7 @@
     )
     far = lax.ppermute(mine, ("zl", "zh"), SWAP_Z)
     near = spread(mine)
-    x_near, sent, top_near = forward(features_of(near), hold(head_weight), head_weight)
+    x_near, *sent, top_near = forward(features_of(near), hold(head_weight), head_weight)
     x_near, far = lax.optimization_barrier((x_near, far))
     first, second = pairing[0], pairing[1]
     which = jnp.where(first == 2, jnp.where(second == 3, 0, 3), jnp.where(first == 3, 1, 2))
@@ -397,7 +415,7 @@
     grads, losses = call(
         grad_kernel,
         [shape(2 * half, vocab, dtype=BF16), shape(8, 2 * half)],
-        (where, whole, local, near, far, x_near, x_far, got_near, got_far),
+        (where, whole, local, near, far, x_near, x_far, *got_near, *got_far),
         "logit_grads",
         [pltpu.VMEM((LANES, half), F32), pltpu.VMEM((half, LANES), F32)],
     )

time: 178 us -> 183 us (1.028)
  starting transfers between devices: 52.4 us -> 61.6 us
  waiting for transfers between devices: 49 us -> 45.8 us
    ppermute x2 -> x4, starting transfers between devices: 6.36 us -> 15 us  [the longest x2 7.63 us: exchange(): got_far = [lax.ppermute(p, 'x', to_learner) for p in sent]]
    ppermute x2 -> x4, waiting for transfers between devices: 9.63 us -> 7.81 us  [the longest x2 3.97 us: exchange(): got_far = [lax.ppermute(p, 'x', to_learner) for p in sent]]
  transfers between devices with their start and end apart: 9 -> 11, of which waited for: 6 -> 7; matrix products, arithmetic and copies ran while one was open for 1% -> 1% of each run, Pallas kernels for 9% -> 9%
where the time goes in v5:
time: 183 us
  starting transfers between devices  61.6 us (34%)
  waiting for transfers between devices  45.8 us (25%)
  blocking collectives  40.4 us (22%)
  Pallas kernels  25.1 us (14%)
  local copies, waits for them, and re-layouts  5.27 us (3%)
  between operations  2.59 us (1%)
    pallas_call x13, Pallas kernels, call(): pl.pallas_call(kernel, out_shape=outs if len(outs) > 1 else outs[0], in_s...  22.1 us
    all_to_all x1, blocking collectives, on_device(): by_y = lax.all_to_all(by_y, 'y', 0, 0)  15.7 us
    all_to_all x1, waiting for transfers between devices, on_device(): by_z = lax.all_to_all(by_z.reshape(16, rows // 8, depth), Z, 0, 0)  12.5 us
    ppermute x1, starting transfers between devices, on_device(): far = lax.ppermute(mine, ('zl', 'zh'), SWAP_Z)  12.4 us
    all_to_all x1, waiting for transfers between devices, on_device(): parts = lax.all_to_all(parts, Z, 0, 0)  12.1 us
    all_to_all x1, starting transfers between devices, on_device(): final = lax.all_to_all(final, 'zl', 0, 0)  9.66 us
    all_to_all x1, waiting for transfers between devices, on_device(): final = lax.all_to_all(final, 'zl', 0, 0)  9.56 us
    all_to_all x2, starting transfers between devices, spread(): lax.all_to_all(jnp.broadcast_to(block[None], (4,) + block.shape), 'y', 0, 0)  9.53 us
  transfers between devices with their start and end apart: 11, of which 7 were waited for; matrix products, arithmetic and copies ran while one was open for 1% of the time, Pallas kernels for 9%

profile of v5, /device:TPU:1, one launch (start us, length us, event | category | flops | bytes accessed | tf_op | source)
XLA Modules:
  0.0 182.7 jit_solution(9377843270449820645)
XLA Ops:
  2.5 5.0 %all-to-all-start.4 = ((bf16[4,64,1024]{2,1,0:T(8,128)(2,1)}), bf16[4,64,1024]{2,1,0:T(8,128)(2,1)S(1)}, u32[]{:S(2)}, u32[]{:S(2)}) async-start(bf16[4,64,1024]{2,1,0:T(8,128)(2,1)} %broadcast_in_dim.28), calls=%async_computation.4 | async-start | bytes 1048576 | tf_op jit(solution)/shard_map/all_to_all | solution.py:341
  7.5 12.4 %collective-permute-start.16 = (bf16[64,1024]{1,0:T(8,128)(2,1)S(1)}, bf16[64,1024]{1,0:T(8,128)(2,1)S(1)}, u32[]{:S(2)}, u32[]{:S(2)}) collective-permute-start(bf16[64,1024]{1,0:T(8,128)(2,1)S(1)} %fusion.1), channel_id=1, source_target_pairs={{0,68},{16,84},{32,100},{48,116},{64,4},{80,20},{96,36},{112,52},{... | collective-permute-start | bytes 393224 | tf_op jit(solution)/shard_map/ppermute | solution.py:398
  24.7 3.3 %all_gather.24.h_ref = bf16[256,1792]{1,0:T(8,128)(2,1)S(1)} all-gather(bf16[256,896]{1,0:T(8,128)(2,1)S(1)} %slice.28), channel_id=1, replica_groups=mesh['x'=4,'zl'=8,'c'=2,'zh'=2,'y'=4] {'c'}, dimensions={1}, use_global_device_ids=true | all-gather | bytes 1376256 | tf_op jit(solution)/shard_map/all_gather | solution.py:134
  28.1 3.2 %logits.9 = (f32[256,1024]{1,0:T(8,128)S(1)}, bf16[128,1024]{1,0:T(8,128)(2,1)}, bf16[144,1024]{1,0:T(8,128)(2,1)}, f32[256,128]{1,0:T(8,128)S(1)}) custom-call(bf16[256,1792]{1,0:T(8,128)(2,1)S(1)} %all_gather.24.h_ref, bf16[896,1024]{1,0:T(8,128)(2,1)S(1)} %hold_head.9.held_ref, bf16[1,1792,1024]{2,1,0:T(8,128)(2,1)} %w_ref.7), custom_call_target="tpu_custom_call" | custom-call | flops 939524096 | bytes 8159232 | tf_op jit(solution)/shard_map/logits/pallas_call | solution.py:30
  31.3 47.9 %conditional.1 = (f32[8,8,512]{2,1,0:T(8,128)S(1)}, bf16[256,1024]{1,0:T(8,128)(2,1)}, f32[256,1024]{1,0:T(8,128)S(1)}, f32[256,1024]{1,0:T(8,128)}, bf16[128,10...) conditional(s32[]{:T(128)} %bitcast.7, ...), branch_computations={%region_0.1_spmd, %region_1.2_spmd, %region_2.3_spmd, %region_3.4_... | conditional | flops 939524096 | bytes 35963208 | solution.py:404
  32.2 4.5 %all-to-all-start = ((bf16[4,64,1024]{2,1,0:T(8,128)(2,1)}), bf16[4,64,1024]{2,1,0:T(8,128)(2,1)}, u32[]{:S(2)}, u32[]{:S(2)}) async-start(bf16[4,64,1024]{2,1,0:T(8,128)(2,1)} %broadcast_in_dim.1), calls=%async_computation | async-start | bytes 1048576 | tf_op jit(solution)/shard_map/cond/branch_0_fun/all_to_all | solution.py:341
  36.7 4.4 %collective-permute-start.1 = (bf16[144,1024]{1,0:T(8,128)(2,1)}, bf16[144,1024]{1,0:T(8,128)(2,1)}, u32[]{:S(2)}, u32[]{:S(2)}) collective-permute-start(bf16[144,1024]{1,0:T(8,128)(2,1)} %get-tuple-element.85), channel_id=1, source_target_pairs={{256,0},{384,128},{128,256},{0,384},{257,1},{385,129},{129,257},{1... | collective-permute-start | bytes 884744 | tf_op jit(solution)/shard_map/cond/branch_0_fun/ppermute | solution.py:355
  46.6 3.7 %all_gather.16.h_ref = bf16[256,1792]{1,0:T(8,128)(2,1)S(1)} all-gather(bf16[256,896]{1,0:T(8,128)(2,1)S(1)} %slice.24), channel_id=1, replica_groups=mesh['x'=4,'zl'=8,'c'=2,'zh'=2,'y'=4] {'c'}, dimensions={1}, use_global_device_ids=true | all-gather | bytes 1376256 | tf_op jit(solution)/shard_map/cond/branch_0_fun/all_gather | solution.py:134
  50.4 3.5 %logits.5 = (f32[256,1024]{1,0:T(8,128)}, bf16[128,1024]{1,0:T(8,128)(2,1)S(1)}, bf16[144,1024]{1,0:T(8,128)(2,1)S(1)}, f32[256,128]{1,0:T(8,128)S(1)}) custom-call(bf16[256,1792]{1,0:T(8,128)(2,1)S(1)} %all_gather.16.h_ref, bf16[896,1024]{1,0:T(8,128)(2,1)S(1)} %hold_head.5.held_ref, bf16[1,1792,1024]{2,1,0:T(8,128)(2,1)} %get-tuple-element.74.w_ref), custom_call_target="tpu_custom_call" | custom-call | flops 939524096 | bytes 8159232 | tf_op jit(solution)/shard_map/cond/branch_0_fun/logits/pallas_call | solution.py:30
  53.9 4.5 %collective-permute-start.3 = (bf16[144,1024]{1,0:T(8,128)(2,1)S(1)}, bf16[144,1024]{1,0:T(8,128)(2,1)}, u32[]{:S(2)}, u32[]{:S(2)}) collective-permute-start(bf16[144,1024]{1,0:T(8,128)(2,1)S(1)} %get-tuple-element.91), channel_id=1, source_target_pairs={{256,0},{384,128},{128,256},{0,384},{257,1},{385,129},{129,257},{1... | collective-permute-start | bytes 884744 | tf_op jit(solution)/shard_map/cond/branch_0_fun/ppermute | solution.py:359
  61.5 3.1 %collective-permute-start.2 = (bf16[128,1024]{1,0:T(8,128)(2,1)S(1)}, bf16[128,1024]{1,0:T(8,128)(2,1)}, u32[]{:S(2)}, u32[]{:S(2)}) collective-permute-start(bf16[128,1024]{1,0:T(8,128)(2,1)S(1)} %get-tuple-element.90), channel_id=1, source_target_pairs={{256,0},{384,128},{128,256},{0,384},{257,1},{385,129},{129,257},{1... | collective-permute-start | bytes 786440 | tf_op jit(solution)/shard_map/cond/branch_0_fun/ppermute | solution.py:359
  67.5 3.8 %collective-permute-done.first_ref = bf16[128,1024]{1,0:T(8,128)(2,1)} collective-permute-done((bf16[128,1024]{1,0:T(8,128)(2,1)S(1)}, bf16[128,1024]{1,0:T(8,128)(2,1)}, u32[]{:S(2)}, u32[]{:S(2)}) %collective-permute-start) | collective-permute-done | bytes 262176 | tf_op jit(solution)/shard_map/cond/branch_0_fun/ppermute | solution.py:355
  73.0 4.0 %collective-permute-done.2.first_ref = bf16[128,1024]{1,0:T(8,128)(2,1)} collective-permute-done((bf16[128,1024]{1,0:T(8,128)(2,1)S(1)}, bf16[128,1024]{1,0:T(8,128)(2,1)}, u32[]{:S(2)}, u32[]{:S(2)}) %collective-permute-start.2) | collective-permute-done | bytes 262176 | tf_op jit(solution)/shard_map/cond/branch_0_fun/ppermute | solution.py:359
  79.2 8.7 %all_to_all.46.in_ref = f32[8,8,512]{2,1,0:T(8,128)S(1)} all-to-all(f32[8,8,512]{2,1,0:T(8,128)S(1)} %get-tuple-element.176.local_ref), channel_id=1, replica_groups=mesh['x'=4,'zl'=8,'c'=2,'zh'=2,'y'=4] {'c','y'}, dimensions={0} | all-to-all | bytes 262144 | tf_op jit(solution)/shard_map/all_to_all | solution.py:410
  88.7 8.6 %all-to-all-start.6 = ((f32[16,8,256]{2,1,0:T(8,128)}), f32[16,8,256]{2,1,0:T(8,128)S(1)}, u32[]{:S(2)}, u32[]{:S(2)}) async-start(f32[16,8,256]{2,1,0:T(8,128)} %merge_near.1), calls=%async_computation.6 | async-start | bytes 262144 | tf_op jit(solution)/shard_map/all_to_all | solution.py:412
  97.3 12.1 %all-to-all-done.6.in_ref = f32[16,8,256]{2,1,0:T(8,128)S(1)} async-done(((f32[16,8,256]{2,1,0:T(8,128)}), f32[16,8,256]{2,1,0:T(8,128)S(1)}, u32[]{:S(2)}, u32[]{:S(2)}) %all-to-all-start.6) | async-done | bytes 131104 | tf_op jit(solution)/shard_map/all_to_all | solution.py:412
  109.5 4.7 %all-gather = f32[16,256]{1,0:T(8,128)S(1)} all-gather(f32[8,256]{1,0:T(8,128)S(1)} %merge_all.1), channel_id=2, replica_groups=mesh['x'=4,'zl'=8,'c'=2,'zh'=2,'y'=4] {'c'}, dimensions={0}, use_global_device_ids=true | all-gather | bytes 24576 | tf_op jit(solution)/shard_map/all_gather | solution.py:414
  114.3 3.9 %logit_grads.1 = (bf16[512,1024]{1,0:T(8,128)(2,1)S(1)}, f32[8,512]{1,0:T(8,128)S(1)}) custom-call(s32[2]{0:T(128)S(1)} %pad_add_fusion.where_ref, f32[2,8,256]{2,1,0:T(8,128)S(1)} %bitcast.24, f32[8,8,512]{2,1,0:T(8,128)S(1)} %get-tuple-element.176.local_ref, bf16[256,1024]{1,0:T(8,128)(2,1)} %bitcast.30, bf16[256,1024]{1,0:T(8,128)(2,1)} %get-tuple-element.177.far_ids, ...), custom_call_target="tpu_custom_call" | custom-call | bytes 5472264 | tf_op jit(solution)/shard_map/logit_grads/pallas_call | solution.py:30
  124.1 15.7 %all_to_all.47.in_ref = bf16[4,128,896]{2,1,0:T(8,128)(2,1)S(1)} all-to-all(bf16[4,128,896]{2,1,0:T(8,128)(2,1)S(1)} %bitcast.31), channel_id=1, replica_groups=mesh['x'=4,'zl'=8,'c'=2,'zh'=2,'y'=4] {'y'}, dimensions={0} | all-to-all | bytes 1835008 | tf_op jit(solution)/shard_map/all_to_all | solution.py:428
  140.6 4.0 %all-to-all-start.8 = ((bf16[16,8,896]{2,1,0:T(8,128)(2,1)}), bf16[16,8,896]{2,1,0:T(8,128)(2,1)S(1)}, u32[]{:S(2)}, u32[]{:S(2)}) async-start(bf16[16,8,896]{2,1,0:T(8,128)(2,1)} %bitcast.15), calls=%async_computation.8 | async-start | bytes 458752 | tf_op jit(solution)/shard_map/all_to_all | solution.py:430
  144.7 12.5 %all-to-all-done.8.in_ref = bf16[16,8,896]{2,1,0:T(8,128)(2,1)S(1)} async-done(((bf16[16,8,896]{2,1,0:T(8,128)(2,1)}), bf16[16,8,896]{2,1,0:T(8,128)(2,1)S(1)}, u32[]{:S(2)}, u32[]{:S(2)}) %all-to-all-start.8) | async-done | bytes 229408 | tf_op jit(solution)/shard_map/all_to_all | solution.py:430
  158.0 9.7 %all-to-all-start.9 = ((bf16[8,8,896]{2,1,0:T(8,128)(2,1)}), bf16[8,8,896]{2,1,0:T(8,128)(2,1)S(1)}, u32[]{:S(2)}, u32[]{:S(2)}) async-start(bf16[8,8,896]{2,1,0:T(8,128)(2,1)} %sum_z.1), calls=%async_computation.9 | async-start | bytes 229376 | tf_op jit(solution)/shard_map/all_to_all | solution.py:438
  168.3 9.6 %all-to-all-done.9 = bf16[8,8,896]{2,1,0:T(8,128)(2,1)S(1)} async-done(((bf16[8,8,896]{2,1,0:T(8,128)(2,1)}), bf16[8,8,896]{2,1,0:T(8,128)(2,1)S(1)}, u32[]{:S(2)}, u32[]{:S(2)}) %all-to-all-start.9) | async-done | bytes 114720 | tf_op jit(solution)/shard_map/all_to_all | solution.py:438
  177.8 4.1 %all_gather.27 = bf16[64,1792]{1,0:T(8,128)(2,1)S(1)} all-gather(bf16[64,896]{1,0:T(8,128)(2,1)S(1)} %bitcast.33), channel_id=1, replica_groups=mesh['x'=4,'zl'=8,'c'=2,'zh'=2,'y'=4] {'c'}, dimensions={1}, use_global_device_ids=true | all-gather | bytes 344064 | tf_op jit(solution)/shard_map/all_gather | solution.py:439
  (50 shorter events, 30.4 us)
Async XLA Ops:
  0.6 1.0 copy-start
  2.5 21.4 %all-to-all-start.4 = ((bf16[4,64,1024]{2,1,0:T(8,128)(2,1)}), bf16[4,64,1024]{2,1,0:T(8,128)(2,1)S(1)}, u32[]{:S(2)}, u32[]{:S(2)}) async-start(bf16[4,64,1024]{2,1,0:T(8,128)(2,1)} %broadcast_in_dim.28), calls=%async_computation.4 | async-start | bytes 1048576 | tf_op jit(solution)/shard_map/all_to_all | solution.py:341
  7.5 23.8 %collective-permute-start.16 = (bf16[64,1024]{1,0:T(8,128)(2,1)S(1)}, bf16[64,1024]{1,0:T(8,128)(2,1)S(1)}, u32[]{:S(2)}, u32[]{:S(2)}) collective-permute-start(bf16[64,1024]{1,0:T(8,128)(2,1)S(1)} %fusion.1), channel_id=1, source_target_pairs={{0,68},{16,84},{32,100},{48,116},{64,4},{80,20},{96,36},{112,52},{... | collective-permute-start | bytes 393224 | tf_op jit(solution)/shard_map/ppermute | solution.py:398
  20.0 1.5 copy-start.7
  23.9 0.8 copy-start.2
  32.2 13.4 %all-to-all-start = ((bf16[4,64,1024]{2,1,0:T(8,128)(2,1)}), bf16[4,64,1024]{2,1,0:T(8,128)(2,1)}, u32[]{:S(2)}, u32[]{:S(2)}) async-start(bf16[4,64,1024]{2,1,0:T(8,128)(2,1)} %broadcast_in_dim.1), calls=%async_computation | async-start | bytes 1048576 | tf_op jit(solution)/shard_map/cond/branch_0_fun/all_to_all | solution.py:341
  36.7 34.7 %collective-permute-start.1 = (bf16[144,1024]{1,0:T(8,128)(2,1)}, bf16[144,1024]{1,0:T(8,128)(2,1)}, u32[]{:S(2)}, u32[]{:S(2)}) collective-permute-start(bf16[144,1024]{1,0:T(8,128)(2,1)} %get-tuple-element.85), channel_id=1, source_target_pairs={{256,0},{384,128},{128,256},{0,384},{257,1},{385,129},{129,257},{1... | collective-permute-start | bytes 884744 | tf_op jit(solution)/shard_map/cond/branch_0_fun/ppermute | solution.py:355
  50.4 8.0 %copy-start.9 = (bf16[128,1024]{1,0:T(8,128)(2,1)S(1)}, bf16[128,1024]{1,0:T(8,128)(2,1)}, u32[]{:S(2)}) copy-start(bf16[128,1024]{1,0:T(8,128)(2,1)} %get-tuple-element.84) | copy-start | bytes 786436 | tf_op jit(solution)/shard_map/cond
  53.9 12.9 %copy-start.3 = (bf16[256,1024]{1,0:T(8,128)(2,1)S(1)}, bf16[256,1024]{1,0:T(8,128)(2,1)}, u32[]{:S(2)}) copy-start(bf16[256,1024]{1,0:T(8,128)(2,1)} %get-tuple-element.80.ids_ref) | copy-start | bytes 1572868 | tf_op jit(solution)/shard_map/cond
  53.9 23.1 %collective-permute-start.3 = (bf16[144,1024]{1,0:T(8,128)(2,1)S(1)}, bf16[144,1024]{1,0:T(8,128)(2,1)}, u32[]{:S(2)}, u32[]{:S(2)}) collective-permute-start(bf16[144,1024]{1,0:T(8,128)(2,1)S(1)} %get-tuple-element.91), channel_id=1, source_target_pairs={{256,0},{384,128},{128,256},{0,384},{257,1},{385,129},{129,257},{1... | collective-permute-start | bytes 884744 | tf_op jit(solution)/shard_map/cond/branch_0_fun/ppermute | solution.py:359
  58.4 12.9 %collective-permute-start = (bf16[128,1024]{1,0:T(8,128)(2,1)S(1)}, bf16[128,1024]{1,0:T(8,128)(2,1)}, u32[]{:S(2)}, u32[]{:S(2)}) collective-permute-start(bf16[128,1024]{1,0:T(8,128)(2,1)S(1)} %copy-done.9), channel_id=1, source_target_pairs={{256,0},{384,128},{128,256},{0,384},{257,1},{385,129},{129,257},{1... | collective-permute-start | bytes 786440 | tf_op jit(solution)/shard_map/cond/branch_0_fun/ppermute | solution.py:355
  61.5 15.5 %collective-permute-start.2 = (bf16[128,1024]{1,0:T(8,128)(2,1)S(1)}, bf16[128,1024]{1,0:T(8,128)(2,1)}, u32[]{:S(2)}, u32[]{:S(2)}) collective-permute-start(bf16[128,1024]{1,0:T(8,128)(2,1)S(1)} %get-tuple-element.90), channel_id=1, source_target_pairs={{256,0},{384,128},{128,256},{0,384},{257,1},{385,129},{129,257},{1... | collective-permute-start | bytes 786440 | tf_op jit(solution)/shard_map/cond/branch_0_fun/ppermute | solution.py:359
  88.7 20.8 %all-to-all-start.6 = ((f32[16,8,256]{2,1,0:T(8,128)}), f32[16,8,256]{2,1,0:T(8,128)S(1)}, u32[]{:S(2)}, u32[]{:S(2)}) async-start(f32[16,8,256]{2,1,0:T(8,128)} %merge_near.1), calls=%async_computation.6 | async-start | bytes 262144 | tf_op jit(solution)/shard_map/all_to_all | solution.py:412
  114.3 3.9 %copy-start.1 = (bf16[1,1792,1024]{2,1,0:T(8,128)(2,1)S(1)}, bf16[1,1792,1024]{2,1,0:T(8,128)(2,1)}, u32[]{:S(2)}) copy-start(bf16[1,1792,1024]{2,1,0:T(8,128)(2,1)} %w_ref.7) | copy-start | bytes 11010052
  119.5 4.4 %collective-permute-start.17 = (bf16[512,896]{1,0:T(8,128)(2,1)S(1)}, bf16[512,896]{1,0:T(8,128)(2,1)S(1)}, u32[]{:S(2)}, u32[]{:S(2)}) collective-permute-start(bf16[512,896]{1,0:T(8,128)(2,1)S(1)} %head_grads.3), channel_id=1, source_target_pairs={{0,8},{8,0},{1,9},{9,1},{2,10},{10,2},{3,11},{11,3},{4,12},{12,4},... | collective-permute-start | bytes 2752520 | tf_op jit(solution)/shard_map/ppermute | solution.py:425
  124.0 20.6 %copy-start.8 = (f32[1,64]{1,0:T(1,128)S(1)}, f32[1,64]{1,0:T(1,128)}, u32[]{:S(2)}) copy-start(f32[1,64]{1,0:T(1,128)} %param.13) | copy-start | bytes 772
  140.6 16.6 %all-to-all-start.8 = ((bf16[16,8,896]{2,1,0:T(8,128)(2,1)}), bf16[16,8,896]{2,1,0:T(8,128)(2,1)S(1)}, u32[]{:S(2)}, u32[]{:S(2)}) async-start(bf16[16,8,896]{2,1,0:T(8,128)(2,1)} %bitcast.15), calls=%async_computation.8 | async-start | bytes 458752 | tf_op jit(solution)/shard_map/all_to_all | solution.py:430
  158.0 19.8 %all-to-all-start.9 = ((bf16[8,8,896]{2,1,0:T(8,128)(2,1)}), bf16[8,8,896]{2,1,0:T(8,128)(2,1)S(1)}, u32[]{:S(2)}, u32[]{:S(2)}) async-start(bf16[8,8,896]{2,1,0:T(8,128)(2,1)} %sum_z.1), calls=%async_computation.9 | async-start | bytes 229376 | tf_op jit(solution)/shard_map/all_to_all | solution.py:438
